TPU v7x, 32 devices: a whole 2x2x4 slice. The times are simulated.
32 devices in a mesh: seq: 16 (over z, y, x), tp: 2 (over core).
Axes of the slice: x: 2, y: 2, z: 4, core: 2. Of those that a mesh axis runs over, the one named last changes fastest.
Arguments:
- queries: bfloat16 [4096, 8192], P('seq', 'tp'), may hold values from -24 to 24
- keys: bfloat16 [4096, 1024], P('seq', 'tp'), may hold values from -24 to 24
- values: bfloat16 [4096, 1024], P('seq', 'tp'), may hold values from -500 to 500
- doc_ids: int32 [4096], P('seq'), may hold values from 0 to 3, never falling along the last dimension, each value on 1 to 2048 neighbouring positions
- features: bfloat16 [2048, 4096], P('seq'), may hold values from -6 to 6
- projector: bfloat16 [4096, 8192], P('seq', 'tp'), may hold values from -6 to 6
- span_start: int32 [2048], P('seq'), may hold values from 0 to 4092, as said below
- span_len: int32 [2048], P('seq'), may hold values from 1 to 4
- counts: int32 [16], replicated, may hold values from 64 to 128
Outputs:
- targets: bfloat16 [2048, 8192], P('seq', 'tp')
- projector_new: float32 [4096, 8192], P('seq', 'tp')
Inputs may be any that keep to these rules, and one draw needn't show every extreme that they name: `span_start`: slots d * 128 to (d + 1) * 128 - 1 belong to index d of seq and the first counts[d] of them are live. Live starts increase within an index and lie in teacher rows d * 256 to (d + 1) * 256 - 1; a live span ends at most 3 rows past that block and never past row 4095. Slots that are not live hold start d * 256 and length 1.
All inputs are finite; a program needn't handle non-finite values.
Results may differ from a plain program's by a relative error of at most 0.017.
Values may be sent and summed in bfloat16 or wider, within the bound.
A program may use at most 192 MiB of HBM per device.

v0:
```python
import math

import jax
import jax.numpy as jnp
from jax import lax
from jax.sharding import PartitionSpec as P

HD = 128
MAXSPAN = 4


eta_step = 0.5
ridge_weight = 0.1
norm_eps = 1e-06
neg_large = -1e30
far_position = 1 << 30


def passed_along(block, axis, distance):
    devices = range(lax.axis_size(axis))
    route = [(i - distance, i) for i in devices if i - distance in devices]
    return lax.ppermute(block, axis, route)


def attend_block(
    softmax_state, query_grid, query_pos, query_doc, key_block, value_block, key_pos, key_doc
):
    run_max, run_total, run_sum = softmax_state
    scores = jnp.einsum("tkgd,ukd->kgtu", query_grid, key_block, preferred_element_type=jnp.float32)
    scores = scores * query_grid.shape[3] ** (-0.5)
    visible = (key_doc[None, :] == query_doc[:, None]) & (key_pos[None, :] <= query_pos[:, None])
    scores = jnp.where(visible, scores, neg_large)
    new_max = jnp.maximum(run_max, jnp.max(scores, axis=3))
    weights = jnp.where(visible, jnp.exp(scores - new_max[..., None]), 0.0)
    factor = jnp.exp(run_max - new_max)
    run_total = run_total * factor + jnp.sum(weights, axis=3)
    weighted = jnp.einsum(
        "kgtu,ukd->kgtd",
        weights.astype(jnp.bfloat16),
        value_block,
        preferred_element_type=jnp.float32,
    )
    run_sum = run_sum * factor[..., None] + weighted
    return (new_max, run_total, run_sum)


def attend_rows(softmax_state, query_grid, query_pos, query_doc, key_rows, value_rows, doc_rows):
    row_total = key_rows.shape[0]
    block_rows = math.gcd(row_total, 1024)
    block_count = row_total // block_rows
    kv_heads = query_grid.shape[1]
    head_size = query_grid.shape[3]
    key_blocks = key_rows.reshape(block_count, block_rows, kv_heads, head_size)
    value_blocks = value_rows.reshape(block_count, block_rows, kv_heads, head_size)
    doc_blocks = doc_rows.reshape(block_count, block_rows)
    pos_blocks = jnp.arange(row_total, dtype=jnp.int32).reshape(block_count, block_rows)
    pos_blocks = jnp.where(True, pos_blocks, far_position)

    def advance(carried, blocks):
        return (
            attend_block(
                carried,
                query_grid,
                query_pos,
                query_doc,
                blocks[0],
                blocks[1],
                blocks[3],
                blocks[2],
            ),
            None,
        )

    softmax_state, _ = lax.scan(
        advance, softmax_state, (key_blocks, value_blocks, doc_blocks, pos_blocks)
    )
    return softmax_state


def shards(queries, keys, values, doc_ids, features, projector, span_start, span_len, counts):
    tok_count = queries.shape[0]
    kv_heads = keys.shape[1] // HD
    groups = queries.shape[1] // (kv_heads * HD)
    seq_index = lax.axis_index("seq")
    first_row = seq_index * tok_count
    query_grid = queries.reshape(tok_count, kv_heads, groups, HD)
    query_pos = first_row + jnp.arange(tok_count, dtype=jnp.int32)
    softmax_state = (
        jnp.full((kv_heads, groups, tok_count), neg_large, jnp.float32),
        jnp.zeros((kv_heads, groups, tok_count), jnp.float32),
        jnp.zeros((kv_heads, groups, tok_count, HD), jnp.float32),
    )
    softmax_state = attend_rows(
        softmax_state,
        query_grid,
        query_pos,
        doc_ids,
        lax.all_gather(keys, "seq", axis=0, tiled=True),
        lax.all_gather(values, "seq", axis=0, tiled=True),
        lax.all_gather(doc_ids, "seq", axis=0, tiled=True),
    )
    run_max, run_total, run_sum = softmax_state
    attended = (
        (run_sum / run_total[..., None])
        .transpose(2, 0, 1, 3)
        .reshape(tok_count, kv_heads * groups * HD)
        .astype(jnp.bfloat16)
    )
    rim_rows = passed_along(attended[: MAXSPAN - 1], "seq", -1)
    extended = jnp.concatenate([attended, rim_rows], axis=0)
    offsets = span_start - first_row
    columns = jnp.arange(extended.shape[0], dtype=jnp.int32)
    one_hot = (
        (columns[None, :] >= offsets[:, None]) & (columns[None, :] < (offsets + span_len)[:, None])
    ).astype(jnp.bfloat16)
    span_sum = jnp.dot(one_hot, extended, preferred_element_type=jnp.float32)
    slot_count = features.shape[0]
    is_live = jnp.arange(slot_count, dtype=jnp.int32) < lax.dynamic_index_in_dim(
        counts, seq_index, keepdims=False
    )
    span_mean = jnp.where(is_live[:, None], span_sum / span_len[:, None].astype(jnp.float32), 0.0)
    row_sq = lax.psum(jnp.sum(span_mean * span_mean, axis=1), "tp")
    mean_sq = row_sq / (span_mean.shape[1] * lax.axis_size("tp"))
    targets = (span_mean * lax.rsqrt(mean_sq + norm_eps)[:, None]).astype(jnp.bfloat16)
    col_block = features
    prediction = jnp.dot(
        col_block,
        lax.all_gather(projector, "seq", axis=0, tiled=True),
        preferred_element_type=jnp.float32,
    )
    prediction = prediction * features.shape[1] ** (-0.5)
    errors = jnp.where(is_live[:, None], targets.astype(jnp.float32) - prediction, 0.0).astype(
        jnp.bfloat16
    )
    col_block = features
    gram_term = lax.dot_general(
        col_block, errors, (((0,), (0,)), ((), ())), preferred_element_type=jnp.float32
    )
    gram_sum = lax.psum_scatter(
        lax.optimization_barrier(gram_term.astype(jnp.bfloat16))
        .astype(jnp.float32)
        .astype(jnp.bfloat16),
        "seq",
        scatter_dimension=0,
        tiled=True,
    ).astype(jnp.float32)
    live_total = jnp.sum(counts).astype(jnp.float32)
    projector_wide = projector.astype(jnp.float32)
    projector_new = projector_wide + eta_step * (
        math.sqrt(features.shape[1]) * gram_sum / live_total - ridge_weight * projector_wide
    )
    return (targets, projector_new)


def solution(mesh):
    in_specs = (
        P("seq", "tp"),
        P("seq", "tp"),
        P("seq", "tp"),
        P("seq"),
        P("seq", None),
        P("seq", "tp"),
        P("seq"),
        P("seq"),
        P(),
    )
    out_specs = (P("seq", "tp"), P("seq", "tp"))
    return jax.shard_map(shards, mesh=mesh, in_specs=in_specs, out_specs=out_specs, check_vma=False)
```

profile of v0, /device:TPU:12, one launch (start us, length us, event | category | flops | bytes accessed | tf_op | source)
XLA Modules:
  0.0 1248.0 jit_solution(18295178240324851425)
XLA Ops:
  16.7 30.9 %all-gather = s32[16,1,256]{2,1,0:T(1,128)S(1)} all-gather(s32[1,1,256]{2,1,0:T(1,128)S(1)} %bitcast.70), channel_id=1, replica_groups=mesh['seq'=16,'tp'=2] {'seq'}, dimensions={0}, use_global_device_ids=true | all-gather | bytes 17408 | tf_op jit(solution)/shard_map/all_gather | solution.py:100
  50.1 38.0 %all-gather.5.cloned.1.call-done = bf16[4096,512]{1,0:T(8,128)(2,1)} async-done(((bf16[256,512]{1,0:T(8,128)(2,1)}), bf16[4096,512]{1,0:T(8,128)(2,1)}) %all-gather.5.cloned.1.call-update) | async-done | bytes 4194320 | tf_op jit(solution)/shard_map/all_gather | solution.py:98
  88.1 6.9 reshape.44
  95.0 70.5 %all-gather.7.cloned.1.call-done = bf16[4096,512]{1,0:T(8,128)(2,1)} async-done(((bf16[256,512]{1,0:T(8,128)(2,1)}), bf16[4096,512]{1,0:T(8,128)(2,1)}) %all-gather.7.cloned.1.call-update) | async-done | bytes 4194320 | tf_op jit(solution)/shard_map/all_gather | solution.py:99
  165.6 7.0 reshape.46
  172.5 207.4 %while.15 = (s32[]{:T(128)}, f32[4,8,256]{2,1,0:T(8,128)S(1)}, f32[4,8,256]{2,1,0:T(8,128)S(1)}, f32[4,8,256,128]{3,2,1,0:T(8,128)}, s32[4,1024]{1,0:T(4,128)S(1...) while((s32[]{:T(128)}, f32[4,8,256]{2,1,0:T(8,128)S(1)}, ...), condition=%wide.region_3.4_spmd.clone, body=%wide.region_0.3_spmd.clone.sunk | while | flops 4407992320 | bytes 156790000 | solution.py:74
  176.2 13.8 %fusion.54 = (f32[4,8,256]{2,1,0:T(8,128)S(1)}, f32[4,1024,256,8]{2,1,3,0:T(8,128)}) fusion(pred[256,1024]{0,1:T(8,128)(4,1)S(1)} %compare_and_fusion.2, bf16[256,4,8,128]{3,0,2,1:T(8,128)(2,1)S(1)} %get-tuple-element.281, bf16[1,1024,4,128]{3,2,1,0:T(4,128)(2,1)S(1)} %get-tuple-element.241), kind=kOutput, calls=%fused_computation.3.clone.1 | convolution fusion | flops 2172641280 | bytes 36995072 | tf_op jit(solution)/shard_map/while/body/eval_jaxpr/tkgd,ukd->kgtu/dot_general | solution.py:29
  190.0 15.8 %fusion.55 = f32[4,8,256]{2,1,0:T(8,128)S(1)} fusion(f32[4,1024,256,8]{2,1,3,0:T(8,128)} %get-tuple-element.243, f32[4,8,256]{2,1,0:T(8,128)S(1)} %select_maximum_fusion.2, pred[256,1024]{0,1:T(8,128)(4,1)S(1)} %compare_and_fusion.2), kind=kLoop, calls=%fused_computation.5.clone.1 | loop fusion | flops 41934848 | bytes 33882112 | tf_op jit(solution)/shard_map/while/body/eval_jaxpr/reduce_sum | solution.py:36
  205.8 15.5 %fusion.57 = f32[4,8,256,128]{3,2,1,0:T(8,128)S(1)} fusion(f32[4,8,256,128]{3,2,1,0:T(8,128)S(1)} %copy-done.4, f32[4,1024,256,8]{2,1,3,0:T(8,128)} %get-tuple-element.243, f32[4,8,256]{2,1,0:T(8,128)S(1)} %select_maximum_fusion.2, pred[256,1024]{0,1:T(8,128)(4,1)S(1)} %compare_and_fusion.2, f32[4,8,256]{2,1,0:T(8,128)S(1)} %get-tuple-element.245, ...), kind=kOutput, calls=%fused_computation.9.clone.1 | convolution fusion | flops 2192572416 | bytes 43319296 | tf_op jit(solution)/shard_map/while/body/eval_jaxpr/kgtu,ukd->kgtd/dot_general | solution.py:37
  226.9 15.1 %fusion.54 = (f32[4,8,256]{2,1,0:T(8,128)S(1)}, f32[4,1024,256,8]{2,1,3,0:T(8,128)}) fusion(pred[256,1024]{0,1:T(8,128)(4,1)S(1)} %compare_and_fusion.2, bf16[256,4,8,128]{3,0,2,1:T(8,128)(2,1)S(1)} %get-tuple-element.281, bf16[1,1024,4,128]{3,2,1,0:T(4,128)(2,1)S(1)} %get-tuple-element.241), kind=kOutput, calls=%fused_computation.3.clone.1 | convolution fusion | flops 2172641280 | bytes 36995072 | tf_op jit(solution)/shard_map/while/body/eval_jaxpr/tkgd,ukd->kgtu/dot_general | solution.py:29
  242.1 15.7 %fusion.55 = f32[4,8,256]{2,1,0:T(8,128)S(1)} fusion(f32[4,1024,256,8]{2,1,3,0:T(8,128)} %get-tuple-element.243, f32[4,8,256]{2,1,0:T(8,128)S(1)} %select_maximum_fusion.2, pred[256,1024]{0,1:T(8,128)(4,1)S(1)} %compare_and_fusion.2), kind=kLoop, calls=%fused_computation.5.clone.1 | loop fusion | flops 41934848 | bytes 33882112 | tf_op jit(solution)/shard_map/while/body/eval_jaxpr/reduce_sum | solution.py:36
  257.9 15.4 %fusion.57 = f32[4,8,256,128]{3,2,1,0:T(8,128)S(1)} fusion(f32[4,8,256,128]{3,2,1,0:T(8,128)S(1)} %copy-done.4, f32[4,1024,256,8]{2,1,3,0:T(8,128)} %get-tuple-element.243, f32[4,8,256]{2,1,0:T(8,128)S(1)} %select_maximum_fusion.2, pred[256,1024]{0,1:T(8,128)(4,1)S(1)} %compare_and_fusion.2, f32[4,8,256]{2,1,0:T(8,128)S(1)} %get-tuple-element.245, ...), kind=kOutput, calls=%fused_computation.9.clone.1 | convolution fusion | flops 2192572416 | bytes 43319296 | tf_op jit(solution)/shard_map/while/body/eval_jaxpr/kgtu,ukd->kgtd/dot_general | solution.py:37
  278.9 13.4 %fusion.54 = (f32[4,8,256]{2,1,0:T(8,128)S(1)}, f32[4,1024,256,8]{2,1,3,0:T(8,128)}) fusion(pred[256,1024]{0,1:T(8,128)(4,1)S(1)} %compare_and_fusion.2, bf16[256,4,8,128]{3,0,2,1:T(8,128)(2,1)S(1)} %get-tuple-element.281, bf16[1,1024,4,128]{3,2,1,0:T(4,128)(2,1)S(1)} %get-tuple-element.241), kind=kOutput, calls=%fused_computation.3.clone.1 | convolution fusion | flops 2172641280 | bytes 36995072 | tf_op jit(solution)/shard_map/while/body/eval_jaxpr/tkgd,ukd->kgtu/dot_general | solution.py:29
  292.3 15.9 %fusion.55 = f32[4,8,256]{2,1,0:T(8,128)S(1)} fusion(f32[4,1024,256,8]{2,1,3,0:T(8,128)} %get-tuple-element.243, f32[4,8,256]{2,1,0:T(8,128)S(1)} %select_maximum_fusion.2, pred[256,1024]{0,1:T(8,128)(4,1)S(1)} %compare_and_fusion.2), kind=kLoop, calls=%fused_computation.5.clone.1 | loop fusion | flops 41934848 | bytes 33882112 | tf_op jit(solution)/shard_map/while/body/eval_jaxpr/reduce_sum | solution.py:36
  308.3 15.4 %fusion.57 = f32[4,8,256,128]{3,2,1,0:T(8,128)S(1)} fusion(f32[4,8,256,128]{3,2,1,0:T(8,128)S(1)} %copy-done.4, f32[4,1024,256,8]{2,1,3,0:T(8,128)} %get-tuple-element.243, f32[4,8,256]{2,1,0:T(8,128)S(1)} %select_maximum_fusion.2, pred[256,1024]{0,1:T(8,128)(4,1)S(1)} %compare_and_fusion.2, f32[4,8,256]{2,1,0:T(8,128)S(1)} %get-tuple-element.245, ...), kind=kOutput, calls=%fused_computation.9.clone.1 | convolution fusion | flops 2192572416 | bytes 43319296 | tf_op jit(solution)/shard_map/while/body/eval_jaxpr/kgtu,ukd->kgtd/dot_general | solution.py:37
  329.3 17.3 %fusion.54 = (f32[4,8,256]{2,1,0:T(8,128)S(1)}, f32[4,1024,256,8]{2,1,3,0:T(8,128)}) fusion(pred[256,1024]{0,1:T(8,128)(4,1)S(1)} %compare_and_fusion.2, bf16[256,4,8,128]{3,0,2,1:T(8,128)(2,1)S(1)} %get-tuple-element.281, bf16[1,1024,4,128]{3,2,1,0:T(4,128)(2,1)S(1)} %get-tuple-element.241), kind=kOutput, calls=%fused_computation.3.clone.1 | convolution fusion | flops 2172641280 | bytes 36995072 | tf_op jit(solution)/shard_map/while/body/eval_jaxpr/tkgd,ukd->kgtu/dot_general | solution.py:29
  346.7 15.7 %fusion.55 = f32[4,8,256]{2,1,0:T(8,128)S(1)} fusion(f32[4,1024,256,8]{2,1,3,0:T(8,128)} %get-tuple-element.243, f32[4,8,256]{2,1,0:T(8,128)S(1)} %select_maximum_fusion.2, pred[256,1024]{0,1:T(8,128)(4,1)S(1)} %compare_and_fusion.2), kind=kLoop, calls=%fused_computation.5.clone.1 | loop fusion | flops 41934848 | bytes 33882112 | tf_op jit(solution)/shard_map/while/body/eval_jaxpr/reduce_sum | solution.py:36
  362.4 15.4 %fusion.57 = f32[4,8,256,128]{3,2,1,0:T(8,128)S(1)} fusion(f32[4,8,256,128]{3,2,1,0:T(8,128)S(1)} %copy-done.4, f32[4,1024,256,8]{2,1,3,0:T(8,128)} %get-tuple-element.243, f32[4,8,256]{2,1,0:T(8,128)S(1)} %select_maximum_fusion.2, pred[256,1024]{0,1:T(8,128)(4,1)S(1)} %compare_and_fusion.2, f32[4,8,256]{2,1,0:T(8,128)S(1)} %get-tuple-element.245, ...), kind=kOutput, calls=%fused_computation.9.clone.1 | convolution fusion | flops 2192572416 | bytes 43319296 | tf_op jit(solution)/shard_map/while/body/eval_jaxpr/kgtu,ukd->kgtd/dot_general | solution.py:37
  379.9 5.3 copy.27
  404.5 112.2 %all-gather.9.cloned.1.call-done = bf16[4096,4096]{1,0:T(8,128)(2,1)} async-done(((bf16[256,4096]{1,0:T(8,128)(2,1)}), bf16[4096,4096]{1,0:T(8,128)(2,1)}) %all-gather.9.cloned.1.call-update) | async-done | bytes 33554448 | tf_op jit(solution)/shard_map/all_gather | solution.py:128
  516.7 26.6 %convert_bitcast_fusion = bf16[4096,4096]{0,1:T(8,128)(2,1)} fusion(bf16[128,4096]{1,0:T(8,128)(2,1)S(1)} %copy-done, bf16[4096,4096]{1,0:T(8,128)(2,1)} %all-gather.9.cloned.1.call-done, bf16[128,4096]{1,0:T(8,128)(2,1)S(1)} %multiply_convert_fusion, pred[128]{0:T(512)(128)(4,1)S(1)} %copy-done.7), kind=kOutput, calls=%fused_computation.26 | convolution fusion | flops 8609333248 | bytes 69206144 | tf_op jit(solution)/shard_map/dot_general | solution.py:136
  548.6 682.1 %reduce-scatter.2.cloned.1.call-done = bf16[256,4096]{0,1:T(8,128)(2,1)} async-done(((bf16[4096,4096]{0,1:T(8,128)(2,1)}), bf16[256,4096]{0,1:T(8,128)(2,1)}) %reduce-scatter.2.cloned.1.call-update) | async-done | bytes 2097168 | tf_op jit(solution)/shard_map/reduce_scatter | solution.py:139
  1230.7 5.3 convert_add_fusion
  1235.9 5.6 copy.31
  (108 shorter events, 58.3 us)
Async XLA Ops:
  7.2 509.5 %copy-start = (bf16[128,4096]{1,0:T(8,128)(2,1)S(1)}, bf16[128,4096]{1,0:T(8,128)(2,1)}, u32[]{:S(2)}) copy-start(bf16[128,4096]{1,0:T(8,128)(2,1)} %param.15) | copy-start | bytes 3145732
  7.2 80.9 %all-gather.5.cloned.1.call-start = ((), (), s32[]{:S(2)}) async-start(), calls=%async_computation.1 | async-start | bytes 4456448 | tf_op jit(solution)/shard_map/all_gather | solution.py:98
  7.9 157.7 %all-gather.7.cloned.1.call-start = ((), (), s32[]{:S(2)}) async-start(), calls=%async_computation.2 | async-start | bytes 4456448 | tf_op jit(solution)/shard_map/all_gather | solution.py:99
  8.7 508.0 %all-gather.9.cloned.1.call-start = ((), (), s32[]{:S(2)}) async-start(), calls=%async_computation.3 | async-start | bytes 35651584 | tf_op jit(solution)/shard_map/all_gather | solution.py:128
  9.4 1221.3 %reduce-scatter.2.cloned.1.call-start = ((), (), s32[]{:S(2)}) async-start(), calls=%async_computation.4 | async-start | bytes 35651584 | tf_op jit(solution)/shard_map/reduce_scatter | solution.py:139
  9.5 7.2 copy-start.6
  9.5 38.2 %copy-start.13 = (s32[16]{0:T(128)S(1)}, s32[16]{0:T(128)}, u32[]{:S(2)}) copy-start(s32[16]{0:T(128)} %param.19) | copy-start | bytes 196
  9.5 40.0 %copy-start.8 = (s32[128]{0:T(128)S(1)}, s32[128]{0:T(128)}, u32[]{:S(2)}) copy-start(s32[128]{0:T(128)} %param.18) | copy-start | bytes 1540
  9.5 40.0 %copy-start.9 = (s32[128]{0:T(128)S(1)}, s32[128]{0:T(128)}, u32[]{:S(2)}) copy-start(s32[128]{0:T(128)} %param.17) | copy-start | bytes 1540
  189.9 15.9 %copy-start.1 = (bf16[1,1024,4,128]{3,2,1,0:T(4,128)(2,1)S(1)}, bf16[1,1024,4,128]{3,2,1,0:T(4,128)(2,1)}, u32[]{:S(2)}) copy-start(bf16[1,1024,4,128]{3,2,1,0:T(4,128)(2,1)} %get-tuple-element.246) | copy-start | bytes 3145732 | tf_op jit(solution)/shard_map/while
  189.9 15.9 %copy-start.4 = (f32[4,8,256,128]{3,2,1,0:T(8,128)S(1)}, f32[4,8,256,128]{3,2,1,0:T(8,128)}, u32[]{:S(2)}) copy-start(f32[4,8,256,128]{3,2,1,0:T(8,128)} %get-tuple-element.263) | copy-start | bytes 12582916 | tf_op jit(solution)/shard_map/while
  242.1 15.8 %copy-start.1 = (bf16[1,1024,4,128]{3,2,1,0:T(4,128)(2,1)S(1)}, bf16[1,1024,4,128]{3,2,1,0:T(4,128)(2,1)}, u32[]{:S(2)}) copy-start(bf16[1,1024,4,128]{3,2,1,0:T(4,128)(2,1)} %get-tuple-element.246) | copy-start | bytes 3145732 | tf_op jit(solution)/shard_map/while
  242.1 15.8 %copy-start.4 = (f32[4,8,256,128]{3,2,1,0:T(8,128)S(1)}, f32[4,8,256,128]{3,2,1,0:T(8,128)}, u32[]{:S(2)}) copy-start(f32[4,8,256,128]{3,2,1,0:T(8,128)} %get-tuple-element.263) | copy-start | bytes 12582916 | tf_op jit(solution)/shard_map/while
  292.3 16.0 %copy-start.1 = (bf16[1,1024,4,128]{3,2,1,0:T(4,128)(2,1)S(1)}, bf16[1,1024,4,128]{3,2,1,0:T(4,128)(2,1)}, u32[]{:S(2)}) copy-start(bf16[1,1024,4,128]{3,2,1,0:T(4,128)(2,1)} %get-tuple-element.246) | copy-start | bytes 3145732 | tf_op jit(solution)/shard_map/while
  292.3 16.0 %copy-start.4 = (f32[4,8,256,128]{3,2,1,0:T(8,128)S(1)}, f32[4,8,256,128]{3,2,1,0:T(8,128)}, u32[]{:S(2)}) copy-start(f32[4,8,256,128]{3,2,1,0:T(8,128)} %get-tuple-element.263) | copy-start | bytes 12582916 | tf_op jit(solution)/shard_map/while
  346.7 15.8 %copy-start.1 = (bf16[1,1024,4,128]{3,2,1,0:T(4,128)(2,1)S(1)}, bf16[1,1024,4,128]{3,2,1,0:T(4,128)(2,1)}, u32[]{:S(2)}) copy-start(bf16[1,1024,4,128]{3,2,1,0:T(4,128)(2,1)} %get-tuple-element.246) | copy-start | bytes 3145732 | tf_op jit(solution)/shard_map/while
  346.7 15.8 %copy-start.4 = (f32[4,8,256,128]{3,2,1,0:T(8,128)S(1)}, f32[4,8,256,128]{3,2,1,0:T(8,128)}, u32[]{:S(2)}) copy-start(f32[4,8,256,128]{3,2,1,0:T(8,128)} %get-tuple-element.263) | copy-start | bytes 12582916 | tf_op jit(solution)/shard_map/while
  388.2 8.3 copy-start.7
  388.2 8.3 copy-start.10
  388.2 8.3 copy-start.11
  388.2 8.3 copy-start.12
  388.6 6.5 collective-permute-start
  404.5 138.8 %copy-start.3 = (bf16[128,4096]{1,0:T(8,128)(2,1)}, bf16[128,4096]{1,0:T(8,128)(2,1)S(1)}, u32[]{:S(2)}) copy-start(bf16[128,4096]{1,0:T(8,128)(2,1)S(1)} %multiply_convert_fusion) | copy-start | bytes 3145732
  544.9 2.4 copy-start.14
  (5 other events, 9.7 us)
Sparse Core Ops, SparseCore 0:
  10.8 77.2 all-gather.4
  90.8 74.6 all-gather.6
  168.3 348.3 all-gather.8
  543.4 687.2 reduce-scatter.1
where the time goes:
time: 1250 us
  waiting for transfers between devices  905 us (72%)
  matrix products  152 us (12%)
  other arithmetic  79.6 us (6%)
  local copies, waits for them, and re-layouts  59.7 us (5%)
  blocking collectives  33.4 us (3%)
  between operations  14.6 us (1%)
    reduce_scatter x1, waiting for transfers between devices, shards(): lax.psum_scatter(lax.optimization_barrier(gram_term.astype(jnp.bfloat16))...  682 us
    all_gather x1, waiting for transfers between devices, shards(): lax.all_gather(projector, 'seq', axis=0, tiled=True)  112 us
    all_gather x1, waiting for transfers between devices, shards(): lax.all_gather(values, 'seq', axis=0, tiled=True)  70.5 us
    reduce_sum x4, other arithmetic, attend_block(): run_total = run_total * factor + jnp.sum(weights, axis=3)  63.1 us
    dot_general x4, matrix products, attend_block(): jnp.einsum('kgtu,ukd->kgtd', weights.astype(jnp.bfloat16), value_block, p...  61.8 us
    dot_general x4, matrix products, attend_block(): jnp.einsum('tkgd,ukd->kgtu', query_grid, key_block, preferred_element_typ...  59.6 us
    all_gather x1, waiting for transfers between devices, shards(): lax.all_gather(keys, 'seq', axis=0, tiled=True)  38 us
    all_gather x1, blocking collectives, shards(): lax.all_gather(doc_ids, 'seq', axis=0, tiled=True)  30.9 us
  transfers between devices with their start and end apart: 5, of which 5 were waited for; matrix products, arithmetic and copies ran while one was open for 20% of the time, Pallas kernels for 0%

commit v1 on v0

v1 whole, which is shorter than its diff:
```python
import functools
import math

import jax
import jax.numpy as jnp
from jax import lax
from jax.experimental import pallas as pl
from jax.experimental.pallas import tpu as pltpu
from jax.sharding import PartitionSpec as P

HD = 128
MAXSPAN = 4
RIM = 16

eta_step = 0.5
ridge_weight = 0.1
norm_eps = 1e-06
neg_large = -1e30

NT = (((1,), (1,)), ((), ()))


def attention_kernel(groups, spot_ref, q_ref, k_ref, vt_ref, start_ref, hot_ref, out_ref,
                     acc, top, total, bias):
    own = spot_ref[0]
    lowest = spot_ref[1]
    tok = q_ref.shape[0]
    rate = HD ** (-0.5) * math.log2(math.e)
    top[...] = jnp.full(top.shape, neg_large, jnp.float32)
    total[...] = jnp.zeros(total.shape, jnp.float32)
    acc[...] = jnp.zeros(acc.shape, jnp.float32)
    query_pos = own * tok + lax.broadcasted_iota(jnp.int32, (tok, tok), 1)

    def advance(step, carry):
        block = own - step
        key_pos = block * tok + lax.broadcasted_iota(jnp.int32, (tok, tok), 0)
        visible = (key_pos >= start_ref[...]) & (key_pos <= query_pos)
        bias[...] = jnp.where(visible, 0.0, neg_large)
        key_block = k_ref[block]
        value_block = vt_ref[block]
        for g in range(groups):
            lanes = slice(g * HD, (g + 1) * HD)
            scores = lax.dot_general(
                key_block, q_ref[:, lanes], NT, preferred_element_type=jnp.float32
            ) + bias[...]
            old_top = top[g:g + 1, :]
            new_top = jnp.maximum(old_top, jnp.max(scores, axis=0, keepdims=True))
            weights = jnp.exp2((scores - new_top) * rate)
            factor = jnp.exp2((old_top - new_top) * rate)
            top[g:g + 1, :] = new_top
            total[g:g + 1, :] = total[g:g + 1, :] * factor + jnp.sum(
                weights, axis=0, keepdims=True
            )
            acc[lanes, :] = acc[lanes, :] * factor + jnp.dot(
                value_block, weights.astype(jnp.bfloat16), preferred_element_type=jnp.float32
            )
        return carry

    lax.fori_loop(0, own - lowest + 1, advance, 0)
    for g in range(groups):
        lanes = slice(g * HD, (g + 1) * HD)
        mixed = (acc[lanes, :] / total[g:g + 1, :]).astype(jnp.bfloat16)
        out_ref[:, lanes] = lax.dot_general(
            hot_ref[...], mixed, NT, preferred_element_type=jnp.float32
        )


def attend(spot, queries, key_blocks, value_blocks, doc_start, one_hot, kv_heads, groups):
    tok = queries.shape[0]
    count = key_blocks.shape[0]
    hot_rows = one_hot.shape[0]
    wide = groups * HD
    return pl.pallas_call(
        functools.partial(attention_kernel, groups),
        out_shape=jax.ShapeDtypeStruct((hot_rows, queries.shape[1]), jnp.float32),
        grid_spec=pltpu.PrefetchScalarGridSpec(
            num_scalar_prefetch=1,
            grid=(kv_heads,),
            in_specs=[
                pl.BlockSpec((tok, wide), lambda i, s: (0, i)),
                pl.BlockSpec((count, tok, HD), lambda i, s: (0, 0, i)),
                pl.BlockSpec((count, HD, tok), lambda i, s: (0, i, 0)),
                pl.BlockSpec((1, tok), lambda i, s: (0, 0)),
                pl.BlockSpec((hot_rows, tok), lambda i, s: (0, 0)),
            ],
            out_specs=pl.BlockSpec((hot_rows, wide), lambda i, s: (0, i)),
            scratch_shapes=[
                pltpu.VMEM((wide, tok), jnp.float32),
                pltpu.VMEM((groups, tok), jnp.float32),
                pltpu.VMEM((groups, tok), jnp.float32),
                pltpu.VMEM((tok, tok), jnp.float32),
            ],
        ),
        compiler_params=pltpu.CompilerParams(vmem_limit_bytes=40 * 1024 * 1024),
        cost_estimate=pl.CostEstimate(
            flops=4 * tok * queries.shape[1] * 2304,
            bytes_accessed=2 * key_blocks.size * 2 + queries.size * 2,
            transcendentals=tok * queries.shape[1] // HD * 2304,
        ),
    )(spot, queries, key_blocks, value_blocks, doc_start, one_hot)


def shards(queries, keys, values, doc_ids, features, projector, span_start, span_len, counts):
    tok = queries.shape[0]
    kv_heads = keys.shape[1] // HD
    groups = queries.shape[1] // (kv_heads * HD)
    slots = features.shape[0]
    seq_index = lax.axis_index("seq")
    seq_size = lax.axis_size("seq")
    first_row = seq_index * tok

    key_blocks = lax.all_gather(keys, "seq")
    value_blocks = lax.all_gather(values.T, "seq")
    all_docs = lax.all_gather(doc_ids, "seq", axis=0, tiled=True)
    all_features = lax.all_gather(features, "seq", axis=0, tiled=True)
    columns = lax.all_to_all(projector, "seq", split_axis=1, concat_axis=0, tiled=True)

    doc_start = jnp.sum((all_docs[None, :] < doc_ids[:, None]).astype(jnp.int32), axis=1)
    spot = jnp.stack([seq_index.astype(jnp.int32), doc_start[0] // tok])
    offsets = span_start - first_row
    places = jnp.arange(tok + RIM, dtype=jnp.int32)
    one_hot = (
        (places[None, :] >= offsets[:, None]) & (places[None, :] < (offsets + span_len)[:, None])
    ).astype(jnp.bfloat16)
    picks = (jnp.arange(RIM)[:, None] == jnp.arange(tok)[None, :]).astype(jnp.bfloat16)
    hot = jnp.concatenate([one_hot[:, :tok], picks], axis=0)
    pooled = attend(
        spot, queries, key_blocks, value_blocks, doc_start[None, :], hot, kv_heads, groups
    )
    route = [(i + 1, i) for i in range(seq_size - 1)]
    rim = lax.ppermute(pooled[slots:].astype(jnp.bfloat16), "seq", route)
    span_sum = pooled[:slots] + jnp.dot(
        one_hot[:, tok:], rim, preferred_element_type=jnp.float32
    )
    is_live = jnp.arange(slots, dtype=jnp.int32) < lax.dynamic_index_in_dim(
        counts, seq_index, keepdims=False
    )
    span_mean = jnp.where(is_live[:, None], span_sum / span_len[:, None].astype(jnp.float32), 0.0)
    row_sq = lax.psum(jnp.sum(span_mean * span_mean, axis=1), "tp")
    mean_sq = row_sq / (span_mean.shape[1] * lax.axis_size("tp"))
    targets = (span_mean * lax.rsqrt(mean_sq + norm_eps)[:, None]).astype(jnp.bfloat16)

    all_slots = seq_size * slots
    slot_ids = jnp.arange(all_slots, dtype=jnp.int32)
    all_live = slot_ids % slots < jnp.repeat(counts, slots, total_repeat_length=all_slots)
    prediction = jnp.dot(all_features, columns, preferred_element_type=jnp.float32)
    prediction = prediction * features.shape[1] ** (-0.5)
    target_columns = lax.all_to_all(targets, "seq", split_axis=1, concat_axis=0, tiled=True)
    errors = jnp.where(
        all_live[:, None], target_columns.astype(jnp.float32) - prediction, 0.0
    ).astype(jnp.bfloat16)
    gram = lax.dot_general(
        all_features, errors, (((0,), (0,)), ((), ())), preferred_element_type=jnp.float32
    ).astype(jnp.bfloat16)
    gram_sum = lax.all_to_all(gram, "seq", split_axis=0, concat_axis=1, tiled=True)
    live_total = jnp.sum(counts).astype(jnp.float32)
    projector_wide = projector.astype(jnp.float32)
    projector_new = projector_wide + eta_step * (
        math.sqrt(features.shape[1]) * gram_sum.astype(jnp.float32) / live_total
        - ridge_weight * projector_wide
    )
    return (targets, projector_new)


def solution(mesh):
    in_specs = (
        P("seq", "tp"),
        P("seq", "tp"),
        P("seq", "tp"),
        P("seq"),
        P("seq", None),
        P("seq", "tp"),
        P("seq"),
        P("seq"),
        P(),
    )
    out_specs = (P("seq", "tp"), P("seq", "tp"))
    return jax.shard_map(shards, mesh=mesh, in_specs=in_specs, out_specs=out_specs, check_vma=False)
```

time: 1250 us -> 520 us (0.42)
  waiting for transfers between devices: 905 us -> 238 us
  matrix products: 152 us -> 29.9 us
  blocking collectives: 33.4 us -> 93.7 us
  other arithmetic: 79.6 us -> 20.6 us
  starting transfers between devices: 3.7 us -> 57 us
  Pallas kernels: 0 us -> 32 us
  local copies, waits for them, and re-layouts: 59.7 us -> 30.2 us
    reduce_scatter x1 -> x0, waiting for transfers between devices: 682 us -> none  [shards(): lax.psum_scatter(lax.optimization_barrier(gram_term.astype(jnp.bfloat16))...]
    dot_general x10 -> x2, matrix products: 152 us -> 29.9 us  [the longest x1 29.3 us: shards(): lax.dot_general(all_features, errors, (((0,), (0,)), ((), ())), preferred...]
    all_to_all x0 -> x3, waiting for transfers between devices: none -> 88.2 us  [the longest x1 46.9 us: shards(): lax.all_to_all(gram, 'seq', split_axis=0, concat_axis=1, tiled=True)]
    all_gather x3, waiting for transfers between devices: 221 us -> 133 us  [the longest x1 72.6 us: shards(): key_blocks = lax.all_gather(keys, 'seq')]
    reduce_sum x4 -> x1, other arithmetic: 63.1 us -> 0.56 us  [shards(): jnp.sum((all_docs[None, :] < doc_ids[:, None]).astype(jnp.int32), axis=1)]
    all_gather x1, blocking collectives: 30.9 us -> 91.2 us  [shards(): all_docs = lax.all_gather(doc_ids, 'seq', axis=0, tiled=True)]
    all_to_all x0 -> x3, starting transfers between devices: none -> 55 us  [the longest x1 39.2 us: shards(): lax.all_to_all(targets, 'seq', split_axis=1, concat_axis=0, tiled=True)]
    pallas_call x0 -> x1, Pallas kernels: none -> 32 us  [attend(): pl.pallas_call(functools.partial(attention_kernel, groups), out_shape=jax...]
  transfers between devices with their start and end apart: 5 -> 7, of which waited for: 5 -> 6; matrix products, arithmetic and copies ran while one was open for 20% -> 6% of each run, Pallas kernels for 0% -> 6%
where the time goes in v1:
time: 520 us; the launch traced here: 519 us
  waiting for transfers between devices  238 us (46%)
  blocking collectives  93.7 us (18%)
  starting transfers between devices  57 us (11%)
  Pallas kernels  32 us (6%)
  local copies, waits for them, and re-layouts  30.2 us (6%)
  matrix products  29.9 us (6%)
  other arithmetic  20.6 us (4%)
  between operations  17.2 us (3%)
    all_gather x1, blocking collectives, shards(): all_docs = lax.all_gather(doc_ids, 'seq', axis=0, tiled=True)  91.2 us
    all_gather x1, waiting for transfers between devices, shards(): key_blocks = lax.all_gather(keys, 'seq')  72.6 us
    all_gather x1, waiting for transfers between devices, shards(): all_features = lax.all_gather(features, 'seq', axis=0, tiled=True)  57.3 us
    all_to_all x1, waiting for transfers between devices, shards(): lax.all_to_all(gram, 'seq', split_axis=0, concat_axis=1, tiled=True)  46.9 us
    all_to_all x1, waiting for transfers between devices, shards(): lax.all_to_all(targets, 'seq', split_axis=1, concat_axis=0, tiled=True)  41.3 us
    all_to_all x1, starting transfers between devices, shards(): lax.all_to_all(targets, 'seq', split_axis=1, concat_axis=0, tiled=True)  39.2 us
    pallas_call x1, Pallas kernels, attend(): pl.pallas_call(functools.partial(attention_kernel, groups), out_shape=jax...  32 us
    dot_general x1, matrix products, shards(): lax.dot_general(all_features, errors, (((0,), (0,)), ((), ())), preferred...  29.3 us
  transfers between devices with their start and end apart: 7, of which 6 were waited for; matrix products, arithmetic and copies ran while one was open for 6% of the time, Pallas kernels for 6%

profile of v1, /device:TPU:12, one launch (start us, length us, event | category | flops | bytes accessed | tf_op | source)
XLA Modules:
  0.0 518.7 jit_solution(9616199222852499073)
XLA Ops:
  9.4 4.1 copy.29
  13.5 7.3 %all-to-all-start.1 = ((bf16[256,16,256]{0,2,1:T(8,128)(2,1)}), bf16[256,16,256]{0,2,1:T(8,128)(2,1)}, u32[]{:S(2)}, u32[]{:S(2)}) async-start(bf16[256,16,256]{0,2,1:T(8,128)(2,1)} %bitcast.33), calls=%async_computation.1 | async-start | bytes 4194304 | tf_op jit(solution)/shard_map/all_to_all | solution.py:116
  20.8 91.2 %all-gather.2 = s32[16,1,256]{2,1,0:T(1,128)S(1)} all-gather(s32[1,1,256]{2,1,0:T(1,128)S(1)} %bitcast.73), channel_id=1, replica_groups=mesh['seq'=16,'tp'=2] {'seq'}, dimensions={0}, use_global_device_ids=true | all-gather | bytes 17408 | tf_op jit(solution)/shard_map/all_gather | solution.py:114
  116.0 2.7 all-gather.11.cloned.1.call-done
  118.7 6.4 %copy.27 = bf16[8192,256]{1,0:T(8,128)(2,1)} copy(bf16[8192,256]{0,1:T(8,128)(2,1)} %all-gather.11.cloned.1.call-done) | data formatting | bytes 8388608 | tf_op jit(solution)/shard_map/all_gather | solution.py:113
  125.1 72.6 %all-gather.9.cloned.1.call-done = bf16[4096,512]{1,0:T(8,128)(2,1)} async-done(((bf16[256,512]{1,0:T(8,128)(2,1)}), bf16[4096,512]{1,0:T(8,128)(2,1)}) %all-gather.9.cloned.1.call-update) | async-done | bytes 4194320 | tf_op jit(solution)/shard_map/all_gather | solution.py:112
  197.7 2.2 copy-done
  199.9 2.2 copy-done.1
  202.1 32.0 %shard_map.104 = f32[144,4096]{1,0:T(8,128)S(1)} custom-call(s32[2]{0:T(128)S(1)} %pad_add_fusion.spot_ref, bf16[256,4096]{1,0:T(8,128)(2,1)S(1)} %copy-done.2, bf16[16,256,512]{2,1,0:T(8,128)(2,1)S(1)} %bitcast.61, bf16[16,512,256]{2,1,0:T(8,128)(2,1)S(1)} %bitcast.59, s32[1,256]{1,0:T(1,128)S(1)} %bitcast.60, bf16[144,256]{1,0:T(8,128)(2,1)S(1)} %add_convert_fusion.hot_ref), custom_call_target="tpu_custom_call" | custom-call | flops 9663676416 | bytes 10485760 | tf_op jit(solution)/shard_map/pallas_call | solution.py:73
  237.5 15.1 %collective-permute-done = bf16[16,4096]{1,0:T(8,128)(2,1)S(1)} collective-permute-done((bf16[16,4096]{1,0:T(8,128)(2,1)S(1)}, bf16[16,4096]{1,0:T(8,128)(2,1)S(1)}, u32[]{:S(2)}, u32[]{:S(2)}) %collective-permute-start) | collective-permute-done | bytes 131104 | tf_op jit(solution)/shard_map/ppermute | solution.py:131
  253.2 2.5 psum.7
  257.2 39.2 %all-to-all-start = ((bf16[128,16,256]{2,0,1:T(8,128)(2,1)}), bf16[128,16,256]{2,0,1:T(8,128)(2,1)S(1)}, u32[]{:S(2)}, u32[]{:S(2)}) async-start(bf16[128,16,256]{2,0,1:T(8,128)(2,1)} %bitcast.58), calls=%async_computation | async-start | bytes 2097152 | tf_op jit(solution)/shard_map/all_to_all | solution.py:148
  296.4 4.5 compare_select_fusion.1
  301.1 5.7 %fusion.12 = pred[2048]{0:T(1024)(128)(4,1)S(1)} fusion(pred[2048]{0:T(1024)(128)(4,1)S(1)} %get-tuple-element.22, pred[2048]{0:T(1024)(128)(4,1)S(1)} %get-tuple-element.21, pred[2048]{0:T(1024)(128)(4,1)S(1)} %get-tuple-element.20, pred[2048]{0:T(1024)(128)(4,1)S(1)} %get-tuple-element.19, pred[2048]{0:T(1024)(128)(4,1)S(1)} %get-tuple-element.18, ...), kind=kLoop, calls=%fused_computation.46 | loop fusion | flops 51200 | bytes 28708 | tf_op jit(solution)/shard_map/lt | solution.py:145
  306.9 3.9 copy.30
  310.8 41.3 %all-to-all-done = bf16[128,16,256]{2,0,1:T(8,128)(2,1)S(1)} async-done(((bf16[128,16,256]{2,0,1:T(8,128)(2,1)}), bf16[128,16,256]{2,0,1:T(8,128)(2,1)S(1)}, u32[]{:S(2)}, u32[]{:S(2)}) %all-to-all-start) | async-done | bytes 1048608 | tf_op jit(solution)/shard_map/all_to_all | solution.py:148
  352.3 57.3 %all-gather.7.cloned.1.call-done = bf16[2048,4096]{1,0:T(8,128)(2,1)} async-done(((bf16[128,4096]{1,0:T(8,128)(2,1)}), bf16[2048,4096]{1,0:T(8,128)(2,1)}) %all-gather.7.cloned.1.call-update) | async-done | bytes 16777232 | tf_op jit(solution)/shard_map/all_gather | solution.py:115
  409.6 29.3 %convolution_convert_fusion = bf16[256,4096]{1,0:T(8,128)(2,1)} fusion(bf16[2048,4096]{1,0:T(8,128)(2,1)} %all-gather.7.cloned.1.call-done, f32[2048,256]{1,0:T(8,128)S(1)} %bitcast.65, bf16[4096,256]{1,0:T(8,128)(2,1)} %bitcast.66, pred[2048]{0:T(1024)(128)(4,1)S(1)} %fusion.12), kind=kOutput, calls=%fused_computation.2 | convolution fusion | flops 8593080320 | bytes 23070720 | tf_op jit(solution)/shard_map/dot_general | solution.py:152
  438.9 3.1 copy.37
  442.0 8.4 %all-to-all-start.2 = ((bf16[16,256,256]{1,2,0:T(8,128)(2,1)}), bf16[16,256,256]{1,2,0:T(8,128)(2,1)S(1)}, u32[]{:S(2)}, u32[]{:S(2)}) async-start(bf16[16,256,256]{1,2,0:T(8,128)(2,1)} %bitcast.63), calls=%async_computation.2 | async-start | bytes 4194304 | tf_op jit(solution)/shard_map/all_to_all | solution.py:155
  451.8 46.9 %all-to-all-done.2 = bf16[16,256,256]{1,2,0:T(8,128)(2,1)S(1)} async-done(((bf16[16,256,256]{1,2,0:T(8,128)(2,1)}), bf16[16,256,256]{1,2,0:T(8,128)(2,1)S(1)}, u32[]{:S(2)}, u32[]{:S(2)}) %all-to-all-start.2) | async-done | bytes 2097184 | tf_op jit(solution)/shard_map/all_to_all | solution.py:155
  498.8 2.6 multiply_divide_fusion
  501.3 5.8 %copy.32 = f32[256,4096]{1,0:T(8,128)} copy(f32[256,4096]{0,1:T(8,128)} %bitcast.62) | data formatting | bytes 8388608 | tf_op jit(solution)/shard_map/div | solution.py:159
  507.1 5.1 convert_add_fusion
  (44 shorter events, 10.1 us)
Async XLA Ops:
  7.2 111.6 %all-gather.11.cloned.1.call-start = ((), (), s32[]{:S(2)}) async-start(), calls=%async_computation.5 | async-start | bytes 4456448 | tf_op jit(solution)/shard_map/all_gather | solution.py:113
  7.9 189.8 %all-gather.9.cloned.1.call-start = ((), (), s32[]{:S(2)}) async-start(), calls=%async_computation.4 | async-start | bytes 4456448 | tf_op jit(solution)/shard_map/all_gather | solution.py:112
  8.6 400.9 %all-gather.7.cloned.1.call-start = ((), (), s32[]{:S(2)}) async-start(), calls=%async_computation.3 | async-start | bytes 17825792 | tf_op jit(solution)/shard_map/all_gather | solution.py:115
  13.5 7.3 %copy-start.6 = (s32[256]{0:T(256)S(1)}, s32[256]{0:T(256)}, u32[]{:S(2)}) copy-start(s32[256]{0:T(256)} %param.14) | copy-start | bytes 3076
  13.5 102.2 %copy-start.7 = (s32[128]{0:T(128)S(1)}, s32[128]{0:T(128)}, u32[]{:S(2)}) copy-start(s32[128]{0:T(128)} %param.18) | copy-start | bytes 1540
  13.5 102.3 %copy-start.8 = (s32[128]{0:T(128)S(1)}, s32[128]{0:T(128)}, u32[]{:S(2)}) copy-start(s32[128]{0:T(128)} %param.17) | copy-start | bytes 1540
  13.5 243.7 %all-to-all-start.1 = ((bf16[256,16,256]{0,2,1:T(8,128)(2,1)}), bf16[256,16,256]{0,2,1:T(8,128)(2,1)}, u32[]{:S(2)}, u32[]{:S(2)}) async-start(bf16[256,16,256]{0,2,1:T(8,128)(2,1)} %bitcast.33), calls=%async_computation.1 | async-start | bytes 4194304 | tf_op jit(solution)/shard_map/all_to_all | solution.py:116
  116.0 81.7 %copy-start.2 = (bf16[256,4096]{1,0:T(8,128)(2,1)S(1)}, bf16[256,4096]{1,0:T(8,128)(2,1)}, u32[]{:S(2)}) copy-start(bf16[256,4096]{1,0:T(8,128)(2,1)} %q_ref.1) | copy-start | bytes 6291460
  197.7 2.2 copy-start
  199.9 2.2 copy-start.1
  202.1 34.0 %copy-start.5 = (s32[16]{0:T(128)S(1)}, s32[16]{0:T(128)}, u32[]{:S(2)}) copy-start(s32[16]{0:T(128)} %param.19) | copy-start | bytes 196
  234.1 18.4 %collective-permute-start = (bf16[16,4096]{1,0:T(8,128)(2,1)S(1)}, bf16[16,4096]{1,0:T(8,128)(2,1)S(1)}, u32[]{:S(2)}, u32[]{:S(2)}) collective-permute-start(bf16[16,4096]{1,0:T(8,128)(2,1)S(1)} %slice.63), channel_id=1, source_target_pairs={{2,0},{4,2},{6,4},{8,6},{10,8},{12,10},{14,12},{16,14},{18,16},{20... | collective-permute-start | bytes 393224 | tf_op jit(solution)/shard_map/ppermute | solution.py:131
  255.9 1.3 copy-start.4
  257.2 94.8 %all-to-all-start = ((bf16[128,16,256]{2,0,1:T(8,128)(2,1)}), bf16[128,16,256]{2,0,1:T(8,128)(2,1)S(1)}, u32[]{:S(2)}, u32[]{:S(2)}) async-start(bf16[128,16,256]{2,0,1:T(8,128)(2,1)} %bitcast.58), calls=%async_computation | async-start | bytes 2097152 | tf_op jit(solution)/shard_map/all_to_all | solution.py:148
  442.0 56.8 %all-to-all-start.2 = ((bf16[16,256,256]{1,2,0:T(8,128)(2,1)}), bf16[16,256,256]{1,2,0:T(8,128)(2,1)S(1)}, u32[]{:S(2)}, u32[]{:S(2)}) async-start(bf16[16,256,256]{1,2,0:T(8,128)(2,1)} %bitcast.63), calls=%async_computation.2 | async-start | bytes 4194304 | tf_op jit(solution)/shard_map/all_to_all | solution.py:155
  501.3 5.8 %copy-start.3 = (bf16[256,4096]{1,0:T(8,128)(2,1)S(1)}, bf16[256,4096]{1,0:T(8,128)(2,1)}, u32[]{:S(2)}) copy-start(bf16[256,4096]{1,0:T(8,128)(2,1)} %param.16) | copy-start | bytes 6291460
Sparse Core Ops, SparseCore 0:
  10.7 107.9 all-gather.10
  121.5 76.1 all-gather.8
  200.5 209.0 all-gather.6

commit v2 on v1

--- a/solution.py
+++ b/solution.py
@@ -20,7 +20,7 @@
 NT = (((1,), (1,)), ((), ()))
 
 
-def attention_kernel(groups, spot_ref, q_ref, k_ref, vt_ref, start_ref, hot_ref, out_ref,
+def attention_kernel(groups, spot_ref, q_ref, k_ref, v_ref, start_ref, hot_ref, out_ref,
                      acc, top, total, bias):
     own = spot_ref[0]
     lowest = spot_ref[1]
@@ -36,8 +36,8 @@
         key_pos = block * tok + lax.broadcasted_iota(jnp.int32, (tok, tok), 0)
         visible = (key_pos >= start_ref[...]) & (key_pos <= query_pos)
         bias[...] = jnp.where(visible, 0.0, neg_large)
-        key_block = k_ref[block]
-        value_block = vt_ref[block]
+        key_block = k_ref[block, :tok, :]
+        value_block = v_ref[block, :tok, :].T
         for g in range(groups):
             lanes = slice(g * HD, (g + 1) * HD)
             scores = lax.dot_general(
@@ -65,9 +65,9 @@
         )
 
 
-def attend(spot, queries, key_blocks, value_blocks, doc_start, one_hot, kv_heads, groups):
+def attend(spot, queries, mixed_blocks, doc_start, one_hot, kv_heads, groups):
     tok = queries.shape[0]
-    count = key_blocks.shape[0]
+    count, rows = mixed_blocks.shape[:2]
     hot_rows = one_hot.shape[0]
     wide = groups * HD
     return pl.pallas_call(
@@ -78,8 +78,8 @@
             grid=(kv_heads,),
             in_specs=[
                 pl.BlockSpec((tok, wide), lambda i, s: (0, i)),
-                pl.BlockSpec((count, tok, HD), lambda i, s: (0, 0, i)),
-                pl.BlockSpec((count, HD, tok), lambda i, s: (0, i, 0)),
+                pl.BlockSpec((count, rows, HD), lambda i, s: (0, 0, i)),
+                pl.BlockSpec((count, rows, HD), lambda i, s: (0, 0, i + kv_heads)),
                 pl.BlockSpec((1, tok), lambda i, s: (0, 0)),
                 pl.BlockSpec((hot_rows, tok), lambda i, s: (0, 0)),
             ],
@@ -94,10 +94,32 @@
         compiler_params=pltpu.CompilerParams(vmem_limit_bytes=40 * 1024 * 1024),
         cost_estimate=pl.CostEstimate(
             flops=4 * tok * queries.shape[1] * 2304,
-            bytes_accessed=2 * key_blocks.size * 2 + queries.size * 2,
+            bytes_accessed=mixed_blocks.size * 2 + queries.size * 2,
             transcendentals=tok * queries.shape[1] // HD * 2304,
         ),
-    )(spot, queries, key_blocks, value_blocks, doc_start, one_hot)
+    )(spot, queries, mixed_blocks, mixed_blocks, doc_start, one_hot)
+
+
+def step_kernel(depth, total_ref, old_ref, gram_ref, new_ref):
+    wide = old_ref[...].astype(jnp.float32)
+    gram = gram_ref[0].astype(jnp.float32)
+    rate = eta_step * math.sqrt(depth) / total_ref[...]
+    new_ref[...] = wide * (1.0 - eta_step * ridge_weight) + gram * rate
+
+
+def step(projector, gram_sum, live_total, depth):
+    pieces, rows, chunk = gram_sum.shape
+    return pl.pallas_call(
+        functools.partial(step_kernel, depth),
+        out_shape=jax.ShapeDtypeStruct(projector.shape, jnp.float32),
+        grid=(pieces,),
+        in_specs=[
+            pl.BlockSpec((1, 1), lambda i: (0, 0)),
+            pl.BlockSpec((rows, chunk), lambda i: (0, i)),
+            pl.BlockSpec((1, rows, chunk), lambda i: (i, 0, 0)),
+        ],
+        out_specs=pl.BlockSpec((rows, chunk), lambda i: (0, i)),
+    )(live_total.reshape(1, 1), projector, gram_sum)
 
 
 def shards(queries, keys, values, doc_ids, features, projector, span_start, span_len, counts):
@@ -105,15 +127,31 @@
     kv_heads = keys.shape[1] // HD
     groups = queries.shape[1] // (kv_heads * HD)
     slots = features.shape[0]
+    tok_rows = projector.shape[0]
     seq_index = lax.axis_index("seq")
     seq_size = lax.axis_size("seq")
     first_row = seq_index * tok
 
-    key_blocks = lax.all_gather(keys, "seq")
-    value_blocks = lax.all_gather(values.T, "seq")
-    all_docs = lax.all_gather(doc_ids, "seq", axis=0, tiled=True)
-    all_features = lax.all_gather(features, "seq", axis=0, tiled=True)
-    columns = lax.all_to_all(projector, "seq", split_axis=1, concat_axis=0, tiled=True)
+    tp_size = lax.axis_size("tp")
+    tp_index = lax.axis_index("tp")
+    wide = 2 * keys.shape[1]
+    doc_rows = jnp.zeros((RIM, wide), jnp.bfloat16)
+    doc_rows = lax.dynamic_update_slice(doc_rows, doc_ids.astype(jnp.bfloat16)[None, :], (0, 0))
+    mixed = jnp.concatenate([jnp.concatenate([keys, values], axis=1), doc_rows], axis=0)
+    mixed_blocks = lax.all_gather(mixed, "seq")
+    all_docs = mixed_blocks[:, tok, :tok].reshape(-1).astype(jnp.int32)
+    depth = features.shape[1]
+    if tp_size == 2:
+        half = depth // 2
+        part = lax.dynamic_slice_in_dim(features, tp_index * half, half, axis=1)
+    else:
+        part = features
+    part, projector_late, mixed_blocks = lax.optimization_barrier((part, projector, mixed_blocks))
+    near = lax.all_gather(part, "seq", axis=0, tiled=True)
+    chunk = projector.shape[1] // seq_size
+    columns = lax.all_to_all(
+        projector_late.reshape(tok_rows, seq_size, chunk).transpose(1, 0, 2), "seq", 0, 0
+    ).reshape(depth, chunk)
 
     doc_start = jnp.sum((all_docs[None, :] < doc_ids[:, None]).astype(jnp.int32), axis=1)
     spot = jnp.stack([seq_index.astype(jnp.int32), doc_start[0] // tok])
@@ -125,8 +163,9 @@
     picks = (jnp.arange(RIM)[:, None] == jnp.arange(tok)[None, :]).astype(jnp.bfloat16)
     hot = jnp.concatenate([one_hot[:, :tok], picks], axis=0)
     pooled = attend(
-        spot, queries, key_blocks, value_blocks, doc_start[None, :], hot, kv_heads, groups
-    )
+        spot, queries, mixed_blocks, doc_start[None, :], hot, kv_heads, groups
+    )
+    columns, pooled = lax.optimization_barrier((columns, pooled))
     route = [(i + 1, i) for i in range(seq_size - 1)]
     rim = lax.ppermute(pooled[slots:].astype(jnp.bfloat16), "seq", route)
     span_sum = pooled[:slots] + jnp.dot(
@@ -140,26 +179,47 @@
     mean_sq = row_sq / (span_mean.shape[1] * lax.axis_size("tp"))
     targets = (span_mean * lax.rsqrt(mean_sq + norm_eps)[:, None]).astype(jnp.bfloat16)
 
-    all_slots = seq_size * slots
-    slot_ids = jnp.arange(all_slots, dtype=jnp.int32)
-    all_live = slot_ids % slots < jnp.repeat(counts, slots, total_repeat_length=all_slots)
-    prediction = jnp.dot(all_features, columns, preferred_element_type=jnp.float32)
-    prediction = prediction * features.shape[1] ** (-0.5)
-    target_columns = lax.all_to_all(targets, "seq", split_axis=1, concat_axis=0, tiled=True)
+    near, targets_out = lax.optimization_barrier((near, targets))
+    all_live = jnp.arange(slots, dtype=jnp.int32)[None, :] < counts[:, None]
+    if tp_size == 2:
+        far = lax.ppermute(near, "tp", [(0, 1), (1, 0)])
+        near_rows = lax.dynamic_slice_in_dim(columns, tp_index * half, half, axis=0)
+        far_rows = lax.dynamic_slice_in_dim(columns, (1 - tp_index) * half, half, axis=0)
+        prediction = jnp.dot(near, near_rows, preferred_element_type=jnp.float32) + jnp.dot(
+            far, far_rows, preferred_element_type=jnp.float32
+        )
+    else:
+        prediction = jnp.dot(near, columns, preferred_element_type=jnp.float32)
+    prediction = lax.optimization_barrier(prediction * depth ** (-0.5))
+    target_columns = lax.all_to_all(
+        targets.reshape(slots, seq_size, chunk).transpose(1, 0, 2), "seq", 0, 0
+    )
     errors = jnp.where(
-        all_live[:, None], target_columns.astype(jnp.float32) - prediction, 0.0
+        all_live[:, :, None],
+        target_columns.astype(jnp.float32) - prediction.reshape(seq_size, slots, chunk),
+        0.0,
     ).astype(jnp.bfloat16)
-    gram = lax.dot_general(
-        all_features, errors, (((0,), (0,)), ((), ())), preferred_element_type=jnp.float32
-    ).astype(jnp.bfloat16)
-    gram_sum = lax.all_to_all(gram, "seq", split_axis=0, concat_axis=1, tiled=True)
+    errors = lax.optimization_barrier(errors).reshape(seq_size * slots, chunk)
+    over_slots = (((0,), (0,)), ((), ()))
+    gram = lax.dot_general(near, errors, over_slots, preferred_element_type=jnp.float32).astype(
+        jnp.bfloat16
+    )
+    if tp_size == 2:
+        other = lax.dot_general(
+            far, errors, over_slots, preferred_element_type=jnp.float32
+        ).astype(jnp.bfloat16)
+        first = tp_index == 0
+        gram = jnp.concatenate([jnp.where(first, gram, other), jnp.where(first, other, gram)], 0)
+    gram_sum = lax.all_to_all(gram.reshape(seq_size, tok_rows, chunk), "seq", 0, 0)
     live_total = jnp.sum(counts).astype(jnp.float32)
+    if chunk % 128 == 0:
+        return (targets_out, step(projector, gram_sum, live_total, depth))
     projector_wide = projector.astype(jnp.float32)
+    gram_rows = gram_sum.transpose(1, 0, 2).reshape(projector.shape).astype(jnp.float32)
     projector_new = projector_wide + eta_step * (
-        math.sqrt(features.shape[1]) * gram_sum.astype(jnp.float32) / live_total
-        - ridge_weight * projector_wide
-    )
-    return (targets, projector_new)
+        math.sqrt(depth) * gram_rows / live_total - ridge_weight * projector_wide
+    )
+    return (targets_out, projector_new)
 
 
 def solution(mesh):

time: 520 us -> 397 us (0.76)
  blocking collectives: 93.7 us -> 2.44 us
  starting transfers between devices: 57 us -> 20.5 us
  waiting for transfers between devices: 238 us -> 256 us
  local copies, waits for them, and re-layouts: 30.2 us -> 16.7 us
  Pallas kernels: 32 us -> 44.5 us
  other arithmetic: 20.6 us -> 10.7 us
    all_gather x1 -> x0, blocking collectives: 91.2 us -> none  [shards(): all_docs = lax.all_gather(doc_ids, 'seq', axis=0, tiled=True)]
    all_to_all x3, starting transfers between devices: 55 us -> 18.5 us  [the longest x1 6.81 us: shards(): lax.all_to_all(targets.reshape(slots, seq_size, chunk).transpose(1, 0, 2)...]
    all_gather x3 -> x2, waiting for transfers between devices: 133 us -> 152 us  [the longest x1 118 us: shards(): mixed_blocks = lax.all_gather(mixed, 'seq')]
    pallas_call x0 -> x1, Pallas kernels: none -> 11 us  [step(): pl.pallas_call(functools.partial(step_kernel, depth), out_shape=jax.Shape...]
    all_to_all x3, waiting for transfers between devices: 88.2 us -> 97.5 us  [the longest x1 46.5 us: shards(): lax.all_to_all(gram.reshape(seq_size, tok_rows, chunk), 'seq', 0, 0)]
    ppermute x1, waiting for transfers between devices: 15.1 us -> 6.85 us  [shards(): rim = lax.ppermute(pooled[slots:].astype(jnp.bfloat16), 'seq', route)]
    all_gather x1 -> x0, local copies, waits for them, and re-layouts: 6.36 us -> none  [shards(): value_blocks = lax.all_gather(values.T, 'seq')]
    div x1 -> x0, local copies, waits for them, and re-layouts: 5.76 us -> none  [shards(): math.sqrt(features.shape[1]) * gram_sum.astype(jnp.float32) / live_total]
  transfers between devices with their start and end apart: 7 -> 7, of which waited for: 6 -> 6; matrix products, arithmetic and copies ran while one was open for 6% -> 8% of each run, Pallas kernels for 6% -> 8%
where the time goes in v2:
time: 397 us; the launch traced here: 396 us
  waiting for transfers between devices  256 us (64%)
  Pallas kernels  44.5 us (11%)
  matrix products  27.8 us (7%)
  starting transfers between devices  20.5 us (5%)
  between operations  17.4 us (4%)
  local copies, waits for them, and re-layouts  16.7 us (4%)
  other arithmetic  10.7 us (3%)
    all_gather x1, waiting for transfers between devices, shards(): mixed_blocks = lax.all_gather(mixed, 'seq')  118 us
    all_to_all x1, waiting for transfers between devices, shards(): lax.all_to_all(gram.reshape(seq_size, tok_rows, chunk), 'seq', 0, 0)  46.5 us
    all_to_all x1, waiting for transfers between devices, shards(): lax.all_to_all(projector_late.reshape(tok_rows, seq_size, chunk).transpos...  38.2 us
    all_gather x1, waiting for transfers between devices, shards(): near = lax.all_gather(part, 'seq', axis=0, tiled=True)  33.9 us
    pallas_call x1, Pallas kernels, attend(): pl.pallas_call(functools.partial(attention_kernel, groups), out_shape=jax...  33.5 us
    all_to_all x1, waiting for transfers between devices, shards(): lax.all_to_all(targets.reshape(slots, seq_size, chunk).transpose(1, 0, 2)...  12.8 us
    pallas_call x1, Pallas kernels, step(): pl.pallas_call(functools.partial(step_kernel, depth), out_shape=jax.Shape...  11 us
  transfers between devices with their start and end apart: 7, of which 6 were waited for; matrix products, arithmetic and copies ran while one was open for 8% of the time, Pallas kernels for 8%

profile of v2, /device:TPU:12, one launch (start us, length us, event | category | flops | bytes accessed | tf_op | source)
XLA Modules:
  0.0 396.1 jit_solution(6127145427551897406)
XLA Ops:
  8.1 1.9 fusion.7
  11.0 117.9 %all-gather.6.cloned.1.call-done = bf16[4352,1024]{1,0:T(8,128)(2,1)} async-done(((bf16[272,1024]{1,0:T(8,128)(2,1)}), bf16[4352,1024]{1,0:T(8,128)(2,1)}) %all-gather.6.cloned.1.call-update) | async-done | bytes 8912912 | tf_op jit(solution)/shard_map/all_gather | solution.py:141
  128.9 2.5 copy.16
  131.4 6.2 %all-to-all-start = ((bf16[16,256,256]{1,2,0:T(8,128)(2,1)}), bf16[16,256,256]{1,2,0:T(8,128)(2,1)}, u32[]{:S(2)}, u32[]{:S(2)}) async-start(bf16[16,256,256]{1,2,0:T(8,128)(2,1)} %bitcast.3), calls=%async_computation | async-start | bytes 4194304 | tf_op jit(solution)/shard_map/all_to_all | solution.py:152
  142.4 3.5 copy-done.1
  147.5 33.5 %shard_map.104 = f32[144,4096]{1,0:T(8,128)S(1)} custom-call(s32[2]{0:T(128)S(1)} %pad_add_fusion.spot_ref, bf16[256,4096]{1,0:T(8,128)(2,1)S(1)} %copy-done.2, bf16[16,272,1024]{2,1,0:T(8,128)(2,1)S(1)} %bitcast.31, bf16[16,272,1024]{2,1,0:T(8,128)(2,1)S(1)} %bitcast.32, s32[1,256]{1,0:T(1,128)S(1)} %bitcast.29, bf16[144,256]{1,0:T(8,128)(2,1)S(1)} %add_convert_fusion.hot_ref), custom_call_target="tpu_custom_call" | custom-call | flops 9663676416 | bytes 11010048 | tf_op jit(solution)/shard_map/pallas_call | solution.py:73
  181.1 38.2 %all-to-all-done = bf16[16,256,256]{1,2,0:T(8,128)(2,1)} async-done(((bf16[16,256,256]{1,2,0:T(8,128)(2,1)}), bf16[16,256,256]{1,2,0:T(8,128)(2,1)}, u32[]{:S(2)}, u32[]{:S(2)}) %all-to-all-start) | async-done | bytes 2097184 | tf_op jit(solution)/shard_map/all_to_all | solution.py:152
  219.2 3.9 copy.17
  223.8 1.9 collective-permute-start
  227.0 6.8 %collective-permute-done = bf16[16,4096]{1,0:T(8,128)(2,1)} collective-permute-done((bf16[16,4096]{1,0:T(8,128)(2,1)}, bf16[16,4096]{1,0:T(8,128)(2,1)}, u32[]{:S(2)}, u32[]{:S(2)}) %collective-permute-start) | collective-permute-done | bytes 131104 | tf_op jit(solution)/shard_map/ppermute | solution.py:170
  233.8 2.8 multiply_reduce_fusion
  236.6 2.4 psum.7
  239.1 1.8 multiply_convert_fusion
  240.9 33.9 %all-gather.4.cloned.1.call-done = bf16[2048,2048]{1,0:T(8,128)(2,1)} async-done(((bf16[128,2048]{1,0:T(8,128)(2,1)}), bf16[2048,2048]{1,0:T(8,128)(2,1)}) %all-gather.4.cloned.1.call-update) | async-done | bytes 8388624 | tf_op jit(solution)/shard_map/all_gather | solution.py:150
  275.8 6.8 %all-to-all-start.1 = ((bf16[16,128,256]{2,1,0:T(8,128)(2,1)}), bf16[16,128,256]{2,1,0:T(8,128)(2,1)S(1)}, u32[]{:S(2)}, u32[]{:S(2)}) async-start(bf16[16,128,256]{2,1,0:T(8,128)(2,1)} %bitcast.28), calls=%async_computation.1 | async-start | bytes 2097152 | tf_op jit(solution)/shard_map/all_to_all | solution.py:194
  282.7 6.1 %fusion.5 = f32[2048,256]{1,0:T(8,128)S(1)} fusion(bf16[2048,2048]{1,0:T(8,128)(2,1)} %all-gather.4.cloned.1.call-done, bf16[4096,256]{1,0:T(8,128)(2,1)} %bitcast.34, s32[]{:T(128)S(6)} %select_n.36), kind=kOutput, calls=%fused_computation.16 | convolution fusion | flops 2147483648 | bytes 11534340 | tf_op jit(solution)/shard_map/dot_general | solution.py:188
  288.9 7.1 %fusion.2 = f32[2048,256]{1,0:T(8,128)} fusion(f32[2048,256]{1,0:T(8,128)S(1)} %fusion.5, bf16[2048,2048]{1,0:T(8,128)(2,1)} %collective-permute-done.1, bf16[4096,256]{1,0:T(8,128)(2,1)S(1)} %bitcast.35, s32[]{:T(128)S(6)} %select_n.41), kind=kOutput, calls=%fused_computation.5 | convolution fusion | flops 2148532224 | bytes 13631492 | tf_op jit(solution)/shard_map/dot_general | solution.py:188
  295.9 12.8 %all-to-all-done.1 = bf16[16,128,256]{2,1,0:T(8,128)(2,1)S(1)} async-done(((bf16[16,128,256]{2,1,0:T(8,128)(2,1)}), bf16[16,128,256]{2,1,0:T(8,128)(2,1)S(1)}, u32[]{:S(2)}, u32[]{:S(2)}) %all-to-all-start.1) | async-done | bytes 1048608 | tf_op jit(solution)/shard_map/all_to_all | solution.py:194
  308.7 1.8 select_convert_fusion
  310.5 5.9 %convolution_convert_fusion.1 = bf16[2048,256]{1,0:T(8,128)(2,1)S(1)} fusion(bf16[2048,2048]{1,0:T(8,128)(2,1)} %all-gather.4.cloned.1.call-done, bf16[2048,256]{1,0:T(8,128)(2,1)S(1)} %bitcast.37), kind=kOutput, calls=%fused_computation.7 | convolution fusion | flops 2148007936 | bytes 10485760 | tf_op jit(solution)/shard_map/dot_general | solution.py:204
  316.4 5.9 %broadcast_select_fusion.1 = (bf16[2048,256]{1,0:T(8,128)(2,1)S(1)}, bf16[2048,256]{1,0:T(8,128)(2,1)S(1)}) fusion(bf16[2048,256]{1,0:T(8,128)(2,1)S(1)} %convolution_convert_fusion.1, pred[]{:T(512)S(6)} %eq.19, bf16[2048,2048]{1,0:T(8,128)(2,1)} %collective-permute-done.1, bf16[2048,256]{1,0:T(8,128)(2,1)S(1)} %bitcast.38), kind=kOutput, calls=%fused_computation.19 | convolution fusion | flops 2149056512 | bytes 12582913 | tf_op jit(solution)/shard_map/dot_general | solution.py:208
  323.8 5.6 %all-to-all-start.2 = ((bf16[16,256,256]{2,1,0:T(8,128)(2,1)}), bf16[16,256,256]{2,1,0:T(8,128)(2,1)S(1)}, u32[]{:S(2)}, u32[]{:S(2)}) async-start(bf16[16,256,256]{2,1,0:T(8,128)(2,1)} %bitcast.14), calls=%async_computation.2 | async-start | bytes 4194304 | tf_op jit(solution)/shard_map/all_to_all | solution.py:213
  330.5 46.5 %all-to-all-done.2.gram_ref = bf16[16,256,256]{2,1,0:T(8,128)(2,1)S(1)} async-done(((bf16[16,256,256]{2,1,0:T(8,128)(2,1)}), bf16[16,256,256]{2,1,0:T(8,128)(2,1)S(1)}, u32[]{:S(2)}, u32[]{:S(2)}) %all-to-all-start.2) | async-done | bytes 2097184 | tf_op jit(solution)/shard_map/all_to_all | solution.py:213
  378.3 11.0 %shard_map.105 = f32[256,4096]{1,0:T(8,128)} custom-call(f32[1,1]{1,0:T(1,128)} %bitcast.10.total_ref, bf16[256,4096]{1,0:T(8,128)(2,1)} %old_ref.1, bf16[16,256,256]{2,1,0:T(8,128)(2,1)} %copy-done.4), custom_call_target="tpu_custom_call" | custom-call | tf_op jit(solution)/shard_map/pallas_call | solution.py:112
  (47 shorter events, 12.1 us)
Async XLA Ops:
  7.2 2.9 copy-start
  7.2 121.7 %copy-start.3 = (bf16[256,4096]{1,0:T(8,128)(2,1)S(1)}, bf16[256,4096]{1,0:T(8,128)(2,1)}, u32[]{:S(2)}) copy-start(bf16[256,4096]{1,0:T(8,128)(2,1)} %old_ref.1) | copy-start | bytes 6291460
  7.2 121.7 %all-gather.6.cloned.1.call-start = ((), (), s32[]{:S(2)}) async-start(), calls=%async_computation.4 | async-start | bytes 9469952 | tf_op jit(solution)/shard_map/all_gather | solution.py:141
  10.0 264.7 %all-gather.4.cloned.1.call-start = ((), (), s32[]{:S(2)}) async-start(), calls=%async_computation.3 | async-start | bytes 8912896 | tf_op jit(solution)/shard_map/all_gather | solution.py:150
  131.4 6.2 %copy-start.9 = (s32[128]{0:T(128)S(1)}, s32[128]{0:T(128)}, u32[]{:S(2)}) copy-start(s32[128]{0:T(128)} %param.16) | copy-start | bytes 1540
  131.4 6.2 %copy-start.10 = (s32[128]{0:T(128)S(1)}, s32[128]{0:T(128)}, u32[]{:S(2)}) copy-start(s32[128]{0:T(128)} %param.15) | copy-start | bytes 1540
  131.4 7.2 %copy-start.7 = (s32[256]{0:T(256)S(1)}, s32[256]{0:T(256)}, u32[]{:S(2)}) copy-start(s32[256]{0:T(256)} %param.12) | copy-start | bytes 3076
  131.4 87.9 %all-to-all-start = ((bf16[16,256,256]{1,2,0:T(8,128)(2,1)}), bf16[16,256,256]{1,2,0:T(8,128)(2,1)}, u32[]{:S(2)}, u32[]{:S(2)}) async-start(bf16[16,256,256]{1,2,0:T(8,128)(2,1)} %bitcast.3), calls=%async_computation | async-start | bytes 4194304 | tf_op jit(solution)/shard_map/all_to_all | solution.py:152
  142.4 3.5 copy-start.1
  145.9 1.6 copy-start.2
  181.1 44.7 %copy-start.8 = (s32[16]{0:T(128)S(1)}, s32[16]{0:T(128)}, u32[]{:S(2)}) copy-start(s32[16]{0:T(128)} %param.17) | copy-start | bytes 196
  223.8 10.0 %collective-permute-start = (bf16[16,4096]{1,0:T(8,128)(2,1)}, bf16[16,4096]{1,0:T(8,128)(2,1)}, u32[]{:S(2)}, u32[]{:S(2)}) collective-permute-start(bf16[16,4096]{1,0:T(8,128)(2,1)} %slice.35), channel_id=1, source_target_pairs={{2,0},{4,2},{6,4},{8,6},{10,8},{12,10},{14,12},{16,14},{18,16},{20... | collective-permute-start | bytes 393224 | tf_op jit(solution)/shard_map/ppermute | solution.py:170
  240.9 35.0 %copy-start.5 = (bf16[128,4096]{1,0:T(8,128)(2,1)}, bf16[128,4096]{1,0:T(8,128)(2,1)S(1)}, u32[]{:S(2)}) copy-start(bf16[128,4096]{1,0:T(8,128)(2,1)S(1)} %multiply_convert_fusion) | copy-start | bytes 3145732
  274.8 14.1 %collective-permute-start.1 = (bf16[2048,2048]{1,0:T(8,128)(2,1)}, bf16[2048,2048]{1,0:T(8,128)(2,1)}, u32[]{:S(2)}, u32[]{:S(2)}) collective-permute-start(bf16[2048,2048]{1,0:T(8,128)(2,1)} %all-gather.4.cloned.1.call-done), channel_id=1, source_target_pairs={{0,1},{1,0},{2,3},{3,2},{4,5},{5,4},{6,7},{7,6},{8,9},{9,8},{10,11... | collective-permute-start | bytes 25165832 | tf_op jit(solution)/shard_map/ppermute | solution.py:185
  275.8 32.9 %all-to-all-start.1 = ((bf16[16,128,256]{2,1,0:T(8,128)(2,1)}), bf16[16,128,256]{2,1,0:T(8,128)(2,1)S(1)}, u32[]{:S(2)}, u32[]{:S(2)}) async-start(bf16[16,128,256]{2,1,0:T(8,128)(2,1)} %bitcast.28), calls=%async_computation.1 | async-start | bytes 2097152 | tf_op jit(solution)/shard_map/all_to_all | solution.py:194
  282.7 6.1 %copy-start.6 = (bf16[16,256,256]{2,1,0:T(8,128)(2,1)S(1)}, bf16[16,256,256]{2,1,0:T(8,128)(2,1)}, u32[]{:S(2)}) copy-start(bf16[16,256,256]{2,1,0:T(8,128)(2,1)} %copy.17) | copy-start | bytes 6291460
  323.8 53.2 %all-to-all-start.2 = ((bf16[16,256,256]{2,1,0:T(8,128)(2,1)}), bf16[16,256,256]{2,1,0:T(8,128)(2,1)S(1)}, u32[]{:S(2)}, u32[]{:S(2)}) async-start(bf16[16,256,256]{2,1,0:T(8,128)(2,1)} %bitcast.14), calls=%async_computation.2 | async-start | bytes 4194304 | tf_op jit(solution)/shard_map/all_to_all | solution.py:213
  377.0 1.3 copy-start.4
Sparse Core Ops, SparseCore 0:
  11.3 117.5 all-gather.5
  131.6 143.0 all-gather.3

commit v3 on v2

--- a/solution.py
+++ b/solution.py
@@ -31,18 +31,18 @@
     acc[...] = jnp.zeros(acc.shape, jnp.float32)
     query_pos = own * tok + lax.broadcasted_iota(jnp.int32, (tok, tok), 1)
 
-    def advance(step, carry):
-        block = own - step
-        key_pos = block * tok + lax.broadcasted_iota(jnp.int32, (tok, tok), 0)
-        visible = (key_pos >= start_ref[...]) & (key_pos <= query_pos)
-        bias[...] = jnp.where(visible, 0.0, neg_large)
+    def meet(block, masked):
         key_block = k_ref[block, :tok, :]
-        value_block = v_ref[block, :tok, :].T
+        value_block = jnp.concatenate(
+            [v_ref[block, r:r + HD, :] for r in range(0, tok, HD)], axis=1
+        )
         for g in range(groups):
             lanes = slice(g * HD, (g + 1) * HD)
             scores = lax.dot_general(
                 key_block, q_ref[:, lanes], NT, preferred_element_type=jnp.float32
-            ) + bias[...]
+            )
+            if masked:
+                scores = scores + bias[...]
             old_top = top[g:g + 1, :]
             new_top = jnp.maximum(old_top, jnp.max(scores, axis=0, keepdims=True))
             weights = jnp.exp2((scores - new_top) * rate)
@@ -54,6 +54,22 @@
             acc[lanes, :] = acc[lanes, :] * factor + jnp.dot(
                 value_block, weights.astype(jnp.bfloat16), preferred_element_type=jnp.float32
             )
+
+    def advance(step, carry):
+        block = own - step
+        whole = (step > 0) & (block * tok >= spot_ref[2])
+
+        @pl.when(whole)
+        def _():
+            meet(block, False)
+
+        @pl.when(jnp.logical_not(whole))
+        def _():
+            key_pos = block * tok + lax.broadcasted_iota(jnp.int32, (tok, tok), 0)
+            visible = (key_pos >= start_ref[...]) & (key_pos <= query_pos)
+            bias[...] = jnp.where(visible, 0.0, neg_large)
+            meet(block, True)
+
         return carry
 
     lax.fori_loop(0, own - lowest + 1, advance, 0)
@@ -102,7 +118,8 @@
 
 def step_kernel(depth, total_ref, old_ref, gram_ref, new_ref):
     wide = old_ref[...].astype(jnp.float32)
-    gram = gram_ref[0].astype(jnp.float32)
+    gram = jnp.concatenate([gram_ref[i] for i in range(gram_ref.shape[0])], axis=1)
+    gram = gram.astype(jnp.float32)
     rate = eta_step * math.sqrt(depth) / total_ref[...]
     new_ref[...] = wide * (1.0 - eta_step * ridge_weight) + gram * rate
 
@@ -112,13 +129,14 @@
     return pl.pallas_call(
         functools.partial(step_kernel, depth),
         out_shape=jax.ShapeDtypeStruct(projector.shape, jnp.float32),
-        grid=(pieces,),
+        grid=(pieces // 4,),
         in_specs=[
             pl.BlockSpec((1, 1), lambda i: (0, 0)),
-            pl.BlockSpec((rows, chunk), lambda i: (0, i)),
-            pl.BlockSpec((1, rows, chunk), lambda i: (i, 0, 0)),
+            pl.BlockSpec((rows, 4 * chunk), lambda i: (0, i)),
+            pl.BlockSpec((4, rows, chunk), lambda i: (i, 0, 0)),
         ],
-        out_specs=pl.BlockSpec((rows, chunk), lambda i: (0, i)),
+        out_specs=pl.BlockSpec((rows, 4 * chunk), lambda i: (0, i)),
+        compiler_params=pltpu.CompilerParams(vmem_limit_bytes=32 * 1024 * 1024),
     )(live_total.reshape(1, 1), projector, gram_sum)
 
 
@@ -137,7 +155,8 @@
     wide = 2 * keys.shape[1]
     doc_rows = jnp.zeros((RIM, wide), jnp.bfloat16)
     doc_rows = lax.dynamic_update_slice(doc_rows, doc_ids.astype(jnp.bfloat16)[None, :], (0, 0))
-    mixed = jnp.concatenate([jnp.concatenate([keys, values], axis=1), doc_rows], axis=0)
+    turned = values.reshape(tok // HD, HD, kv_heads, HD).transpose(0, 3, 2, 1).reshape(keys.shape)
+    mixed = jnp.concatenate([jnp.concatenate([keys, turned], axis=1), doc_rows], axis=0)
     mixed_blocks = lax.all_gather(mixed, "seq")
     all_docs = mixed_blocks[:, tok, :tok].reshape(-1).astype(jnp.int32)
     depth = features.shape[1]
@@ -154,7 +173,7 @@
     ).reshape(depth, chunk)
 
     doc_start = jnp.sum((all_docs[None, :] < doc_ids[:, None]).astype(jnp.int32), axis=1)
-    spot = jnp.stack([seq_index.astype(jnp.int32), doc_start[0] // tok])
+    spot = jnp.stack([seq_index.astype(jnp.int32), doc_start[0] // tok, doc_start[tok - 1]])
     offsets = span_start - first_row
     places = jnp.arange(tok + RIM, dtype=jnp.int32)
     one_hot = (
@@ -212,7 +231,7 @@
         gram = jnp.concatenate([jnp.where(first, gram, other), jnp.where(first, other, gram)], 0)
     gram_sum = lax.all_to_all(gram.reshape(seq_size, tok_rows, chunk), "seq", 0, 0)
     live_total = jnp.sum(counts).astype(jnp.float32)
-    if chunk % 128 == 0:
+    if chunk % 128 == 0 and seq_size % 4 == 0:
         return (targets_out, step(projector, gram_sum, live_total, depth))
     projector_wide = projector.astype(jnp.float32)
     gram_rows = gram_sum.transpose(1, 0, 2).reshape(projector.shape).astype(jnp.float32)

time: 397 us -> 393 us (0.990)
  waiting for transfers between devices: 256 us -> 243 us
  local copies, waits for them, and re-layouts: 16.7 us -> 21.6 us
    all_to_all x1, waiting for transfers between devices: 38.2 us -> 26.4 us  [shards(): lax.all_to_all(projector_late.reshape(tok_rows, seq_size, chunk).transpos...]
    pallas_call x1, Pallas kernels: 33.5 us -> 43.4 us  [attend(): pl.pallas_call(functools.partial(attention_kernel, groups), out_shape=jax...]
    pallas_call x1, Pallas kernels: 11 us -> 4.82 us  [step(): pl.pallas_call(functools.partial(step_kernel, depth), out_shape=jax.Shape...]
  transfers between devices with their start and end apart: 7 -> 7, of which waited for: 6 -> 6; matrix products, arithmetic and copies ran while one was open for 8% -> 9% of each run, Pallas kernels for 8% -> 11%
where the time goes in v3:
time: 393 us; the launch traced here: 392 us
  waiting for transfers between devices  243 us (62%)
  Pallas kernels  48.2 us (12%)
  matrix products  28.4 us (7%)
  local copies, waits for them, and re-layouts  21.6 us (5%)
  starting transfers between devices  19.1 us (5%)
  between operations  17.5 us (4%)
  other arithmetic  12.4 us (3%)
    all_gather x1, waiting for transfers between devices, shards(): mixed_blocks = lax.all_gather(mixed, 'seq')  117 us
    all_to_all x1, waiting for transfers between devices, shards(): lax.all_to_all(gram.reshape(seq_size, tok_rows, chunk), 'seq', 0, 0)  46.4 us
    pallas_call x1, Pallas kernels, attend(): pl.pallas_call(functools.partial(attention_kernel, groups), out_shape=jax...  43.4 us
    all_gather x1, waiting for transfers between devices, shards(): near = lax.all_gather(part, 'seq', axis=0, tiled=True)  33.6 us
    all_to_all x1, waiting for transfers between devices, shards(): lax.all_to_all(projector_late.reshape(tok_rows, seq_size, chunk).transpos...  26.4 us
    all_to_all x1, waiting for transfers between devices, shards(): lax.all_to_all(targets.reshape(slots, seq_size, chunk).transpose(1, 0, 2)...  12.9 us
  transfers between devices with their start and end apart: 7, of which 6 were waited for; matrix products, arithmetic and copies ran while one was open for 9% of the time, Pallas kernels for 11%

profile of v3, /device:TPU:12, one launch (start us, length us, event | category | flops | bytes accessed | tf_op | source)
XLA Modules:
  0.0 392.3 jit_solution(9014230522249576601)
XLA Ops:
  13.9 116.8 %all-gather.6.cloned.1.call-done = bf16[4352,1024]{1,0:T(8,128)(2,1)} async-done(((bf16[272,1024]{1,0:T(8,128)(2,1)}), bf16[4352,1024]{1,0:T(8,128)(2,1)}) %all-gather.6.cloned.1.call-update) | async-done | bytes 8912912 | tf_op jit(solution)/shard_map/all_gather | solution.py:160
  130.7 2.5 copy.20
  133.2 6.2 %all-to-all-start = ((bf16[16,256,256]{1,2,0:T(8,128)(2,1)}), bf16[16,256,256]{1,2,0:T(8,128)(2,1)}, u32[]{:S(2)}, u32[]{:S(2)}) async-start(bf16[16,256,256]{1,2,0:T(8,128)(2,1)} %bitcast.39), calls=%async_computation | async-start | bytes 4194304 | tf_op jit(solution)/shard_map/all_to_all | solution.py:171
  144.8 3.5 copy-done.3
  149.9 43.4 %shard_map.104 = f32[144,4096]{1,0:T(8,128)S(1)} custom-call(s32[3]{0:T(128)S(1)} %pad_add_fusion.spot_ref, bf16[256,4096]{1,0:T(8,128)(2,1)S(1)} %copy-done.4, bf16[16,272,1024]{2,1,0:T(8,128)(2,1)S(1)} %bitcast.37, bf16[16,272,1024]{2,1,0:T(8,128)(2,1)S(1)} %bitcast.38, s32[1,256]{1,0:T(1,128)S(1)} %bitcast.35, bf16[144,256]{1,0:T(8,128)(2,1)S(1)} %add_convert_fusion.hot_ref), custom_call_target="tpu_custom_call" | custom-call | flops 9663676416 | bytes 11010048 | tf_op jit(solution)/shard_map/pallas_call | solution.py:89
  194.7 26.4 %all-to-all-done = bf16[16,256,256]{1,2,0:T(8,128)(2,1)} async-done(((bf16[16,256,256]{1,2,0:T(8,128)(2,1)}), bf16[16,256,256]{1,2,0:T(8,128)(2,1)}, u32[]{:S(2)}, u32[]{:S(2)}) %all-to-all-start) | async-done | bytes 2097184 | tf_op jit(solution)/shard_map/all_to_all | solution.py:171
  221.1 3.9 %copy.21 = bf16[16,256,256]{2,1,0:T(8,128)(2,1)} copy(bf16[16,256,256]{1,2,0:T(8,128)(2,1)} %all-to-all-done) | data formatting | bytes 4194304 | tf_op jit(solution)/shard_map/all_to_all | solution.py:171
  226.0 1.9 collective-permute-start
  229.2 6.5 %collective-permute-done = bf16[16,4096]{1,0:T(8,128)(2,1)S(1)} collective-permute-done((bf16[16,4096]{1,0:T(8,128)(2,1)S(1)}, bf16[16,4096]{1,0:T(8,128)(2,1)S(1)}, u32[]{:S(2)}, u32[]{:S(2)}) %collective-permute-start) | collective-permute-done | bytes 131104 | tf_op jit(solution)/shard_map/ppermute | solution.py:189
  235.7 3.4 multiply_reduce_fusion
  239.2 2.4 psum.7
  241.6 2.8 multiply_convert_fusion
  244.4 33.6 %all-gather.4.cloned.1.call-done = bf16[2048,2048]{1,0:T(8,128)(2,1)} async-done(((bf16[128,2048]{1,0:T(8,128)(2,1)}), bf16[2048,2048]{1,0:T(8,128)(2,1)}) %all-gather.4.cloned.1.call-update) | async-done | bytes 8388624 | tf_op jit(solution)/shard_map/all_gather | solution.py:169
  278.0 2.3 copy.27
  280.4 5.4 %all-to-all-start.1 = ((bf16[16,128,256]{2,1,0:T(8,128)(2,1)}), bf16[16,128,256]{2,1,0:T(8,128)(2,1)}, u32[]{:S(2)}, u32[]{:S(2)}) async-start(bf16[16,128,256]{2,1,0:T(8,128)(2,1)} %bitcast.42), calls=%async_computation.1 | async-start | bytes 2097152 | tf_op jit(solution)/shard_map/all_to_all | solution.py:213
  285.8 6.1 %fusion.5 = f32[2048,256]{1,0:T(8,128)S(1)} fusion(bf16[2048,2048]{1,0:T(8,128)(2,1)} %all-gather.4.cloned.1.call-done, bf16[4096,256]{1,0:T(8,128)(2,1)} %bitcast.43, s32[]{:T(128)S(6)} %select_n.36), kind=kOutput, calls=%fused_computation.16 | convolution fusion | flops 2147483648 | bytes 11534340 | tf_op jit(solution)/shard_map/dot_general | solution.py:207
  292.0 7.1 %fusion.2 = f32[2048,256]{1,0:T(8,128)} fusion(f32[2048,256]{1,0:T(8,128)S(1)} %fusion.5, bf16[2048,2048]{1,0:T(8,128)(2,1)} %collective-permute-done.1, bf16[4096,256]{1,0:T(8,128)(2,1)S(1)} %bitcast.44, s32[]{:T(128)S(6)} %select_n.41), kind=kOutput, calls=%fused_computation.5 | convolution fusion | flops 2148532224 | bytes 13631492 | tf_op jit(solution)/shard_map/dot_general | solution.py:207
  299.1 12.9 %all-to-all-done.1 = bf16[16,128,256]{2,1,0:T(8,128)(2,1)} async-done(((bf16[16,128,256]{2,1,0:T(8,128)(2,1)}), bf16[16,128,256]{2,1,0:T(8,128)(2,1)}, u32[]{:S(2)}, u32[]{:S(2)}) %all-to-all-start.1) | async-done | bytes 1048608 | tf_op jit(solution)/shard_map/all_to_all | solution.py:213
  311.9 2.1 select_convert_fusion
  314.0 5.9 %convolution_convert_fusion.1 = bf16[2048,256]{1,0:T(8,128)(2,1)S(1)} fusion(bf16[2048,2048]{1,0:T(8,128)(2,1)} %all-gather.4.cloned.1.call-done, bf16[2048,256]{1,0:T(8,128)(2,1)S(1)} %bitcast.49), kind=kOutput, calls=%fused_computation.7 | convolution fusion | flops 2148007936 | bytes 10485760 | tf_op jit(solution)/shard_map/dot_general | solution.py:223
  319.9 5.9 %broadcast_select_fusion.1 = (bf16[2048,256]{1,0:T(8,128)(2,1)S(1)}, bf16[2048,256]{1,0:T(8,128)(2,1)S(1)}) fusion(bf16[2048,256]{1,0:T(8,128)(2,1)S(1)} %convolution_convert_fusion.1, pred[]{:T(512)S(6)} %eq.19, bf16[2048,2048]{1,0:T(8,128)(2,1)} %collective-permute-done.1, bf16[2048,256]{1,0:T(8,128)(2,1)S(1)} %bitcast.50), kind=kOutput, calls=%fused_computation.19 | convolution fusion | flops 2149056512 | bytes 12582913 | tf_op jit(solution)/shard_map/dot_general | solution.py:227
  327.3 5.6 %all-to-all-start.2 = ((bf16[16,256,256]{2,1,0:T(8,128)(2,1)}), bf16[16,256,256]{2,1,0:T(8,128)(2,1)}, u32[]{:S(2)}, u32[]{:S(2)}) async-start(bf16[16,256,256]{2,1,0:T(8,128)(2,1)} %bitcast.40), calls=%async_computation.2 | async-start | bytes 4194304 | tf_op jit(solution)/shard_map/all_to_all | solution.py:232
  334.2 46.4 %all-to-all-done.2.gram_ref = bf16[16,256,256]{2,1,0:T(8,128)(2,1)} async-done(((bf16[16,256,256]{2,1,0:T(8,128)(2,1)}), bf16[16,256,256]{2,1,0:T(8,128)(2,1)}, u32[]{:S(2)}, u32[]{:S(2)}) %all-to-all-start.2) | async-done | bytes 2097184 | tf_op jit(solution)/shard_map/all_to_all | solution.py:232
  380.6 4.8 %shard_map.105 = f32[256,4096]{1,0:T(8,128)} custom-call(f32[1,1]{1,0:T(1,128)} %bitcast.11.total_ref, bf16[256,4096]{1,0:T(8,128)(2,1)S(1)} %copy-done.1, bf16[16,256,256]{2,1,0:T(8,128)(2,1)} %all-to-all-done.2.gram_ref), custom_call_target="tpu_custom_call" | custom-call | tf_op jit(solution)/shard_map/pallas_call | solution.py:129
  (48 shorter events, 17.0 us)
Async XLA Ops:
  7.2 5.9 %copy-start = (bf16[128,4096]{1,0:T(8,128)(2,1)S(1)}, bf16[128,4096]{1,0:T(8,128)(2,1)}, u32[]{:S(2)}) copy-start(bf16[128,4096]{1,0:T(8,128)(2,1)} %param.13) | copy-start | bytes 3145732
  7.2 123.5 %all-gather.6.cloned.1.call-start = ((), (), s32[]{:S(2)}) async-start(), calls=%async_computation.4 | async-start | bytes 9469952 | tf_op jit(solution)/shard_map/all_gather | solution.py:160
  9.0 121.7 %copy-start.1 = (bf16[256,4096]{1,0:T(8,128)(2,1)S(1)}, bf16[256,4096]{1,0:T(8,128)(2,1)}, u32[]{:S(2)}) copy-start(bf16[256,4096]{1,0:T(8,128)(2,1)} %old_ref.1) | copy-start | bytes 6291460
  13.0 265.1 %all-gather.4.cloned.1.call-start = ((), (), s32[]{:S(2)}) async-start(), calls=%async_computation.3 | async-start | bytes 8912896 | tf_op jit(solution)/shard_map/all_gather | solution.py:169
  133.2 6.2 %copy-start.8 = (s32[128]{0:T(128)S(1)}, s32[128]{0:T(128)}, u32[]{:S(2)}) copy-start(s32[128]{0:T(128)} %param.16) | copy-start | bytes 1540
  133.2 6.2 %copy-start.9 = (s32[128]{0:T(128)S(1)}, s32[128]{0:T(128)}, u32[]{:S(2)}) copy-start(s32[128]{0:T(128)} %param.15) | copy-start | bytes 1540
  133.2 7.2 %copy-start.6 = (s32[256]{0:T(256)S(1)}, s32[256]{0:T(256)}, u32[]{:S(2)}) copy-start(s32[256]{0:T(256)} %param.12) | copy-start | bytes 3076
  133.2 87.9 %all-to-all-start = ((bf16[16,256,256]{1,2,0:T(8,128)(2,1)}), bf16[16,256,256]{1,2,0:T(8,128)(2,1)}, u32[]{:S(2)}, u32[]{:S(2)}) async-start(bf16[16,256,256]{1,2,0:T(8,128)(2,1)} %bitcast.39), calls=%async_computation | async-start | bytes 4194304 | tf_op jit(solution)/shard_map/all_to_all | solution.py:171
  144.8 3.5 copy-start.3
  148.3 1.6 copy-start.4
  193.3 1.4 copy-start.2
  194.7 33.3 %copy-start.7 = (s32[16]{0:T(128)S(1)}, s32[16]{0:T(128)}, u32[]{:S(2)}) copy-start(s32[16]{0:T(128)} %param.17) | copy-start | bytes 196
  226.0 9.7 %collective-permute-start = (bf16[16,4096]{1,0:T(8,128)(2,1)S(1)}, bf16[16,4096]{1,0:T(8,128)(2,1)S(1)}, u32[]{:S(2)}, u32[]{:S(2)}) collective-permute-start(bf16[16,4096]{1,0:T(8,128)(2,1)S(1)} %slice.39), channel_id=1, source_target_pairs={{2,0},{4,2},{6,4},{8,6},{10,8},{12,10},{14,12},{16,14},{18,16},{20... | collective-permute-start | bytes 393224 | tf_op jit(solution)/shard_map/ppermute | solution.py:189
  278.0 13.9 %collective-permute-start.1 = (bf16[2048,2048]{1,0:T(8,128)(2,1)}, bf16[2048,2048]{1,0:T(8,128)(2,1)}, u32[]{:S(2)}, u32[]{:S(2)}) collective-permute-start(bf16[2048,2048]{1,0:T(8,128)(2,1)} %all-gather.4.cloned.1.call-done), channel_id=1, source_target_pairs={{0,1},{1,0},{2,3},{3,2},{4,5},{5,4},{6,7},{7,6},{8,9},{9,8},{10,11... | collective-permute-start | bytes 25165832 | tf_op jit(solution)/shard_map/ppermute | solution.py:204
  280.4 31.6 %all-to-all-start.1 = ((bf16[16,128,256]{2,1,0:T(8,128)(2,1)}), bf16[16,128,256]{2,1,0:T(8,128)(2,1)}, u32[]{:S(2)}, u32[]{:S(2)}) async-start(bf16[16,128,256]{2,1,0:T(8,128)(2,1)} %bitcast.42), calls=%async_computation.1 | async-start | bytes 2097152 | tf_op jit(solution)/shard_map/all_to_all | solution.py:213
  285.8 6.1 %copy-start.5 = (bf16[16,256,256]{2,1,0:T(8,128)(2,1)S(1)}, bf16[16,256,256]{2,1,0:T(8,128)(2,1)}, u32[]{:S(2)}) copy-start(bf16[16,256,256]{2,1,0:T(8,128)(2,1)} %copy.21) | copy-start | bytes 6291460
  327.3 53.3 %all-to-all-start.2 = ((bf16[16,256,256]{2,1,0:T(8,128)(2,1)}), bf16[16,256,256]{2,1,0:T(8,128)(2,1)}, u32[]{:S(2)}, u32[]{:S(2)}) async-start(bf16[16,256,256]{2,1,0:T(8,128)(2,1)} %bitcast.40), calls=%async_computation.2 | async-start | bytes 4194304 | tf_op jit(solution)/shard_map/all_to_all | solution.py:232
Sparse Core Ops, SparseCore 0:
  13.1 117.5 all-gather.5
  133.4 144.5 all-gather.3
